TPU v7x, 128 devices: a whole 4x4x4 slice. The times are simulated.
128 devices in a mesh: dp: 32 (over z, y, x_lo), tensor: 4 (over x_hi, core).
Axes of the slice: x: 4 (x_hi: 2, x_lo: 2; x = x_hi * 2 + x_lo), y: 4, z: 4, core: 2. Of those that a mesh axis runs over, the one named last changes fastest.
Arguments:
- tokens: bfloat16 [32, 768, 2048], P('dp', 'tensor'), may hold values from -6 to 6
- cotangent: bfloat16 [32, 768, 2048], P('dp', 'tensor'), may hold values from -6 to 6
- adapter_ids: int32 [32], P('dp'), may hold values from 0 to 7
- norm_gains: bfloat16 [2, 2048], replicated, may hold values from 0.4 to 2.8
- lambda_vectors: float32 [4, 8, 128], P(None, 'tensor'), may hold values from -1.2 to 1.2
- weight_inputs: bfloat16 [3, 2048, 2048], P(None, 'dp', 'tensor'), may hold values from -0.125 to 0.125
- weight_output: bfloat16 [2048, 2048], P('tensor', 'dp'), may hold values from -0.125 to 0.125
- hidden_weight_matrix: bfloat16 [2, 2048, 5632], P(None, 'dp', 'tensor'), may hold values from -0.125 to 0.125
- weight_down: bfloat16 [5632, 2048], P('tensor', 'dp'), may hold values from -0.15625 to 0.15625
- adapter_wide: float32 [7, 128, 2048], P(None, None, ('dp', 'tensor')), may hold values from -0.3125 to 0.3125
- adapter_attention: float32 [4, 128, 2048], P(None, 'dp', 'tensor'), may hold values from -0.3125 to 0.3125
- adapter_feedforward: float32 [3, 128, 5632], P(None, 'dp', 'tensor'), may hold values from -0.3125 to 0.3125
- moment_wide: float32 [7, 128, 2048], P(None, None, ('dp', 'tensor')), may hold values from -0.00030517578 to 0.00030517578
- variance_wide: float32 [7, 128, 2048], P(None, None, ('dp', 'tensor')), may hold values from 1.981661e-10 to 7.926644e-10
- moment_attention: float32 [4, 128, 2048], P(None, 'dp', 'tensor'), may hold values from -0.00030517578 to 0.00030517578
- variance_attention: float32 [4, 128, 2048], P(None, 'dp', 'tensor'), may hold values from 1.981661e-10 to 7.926644e-10
- moment_feedforward: float32 [3, 128, 5632], P(None, 'dp', 'tensor'), may hold values from -0.00030517578 to 0.00030517578
- variance_feedforward: float32 [3, 128, 5632], P(None, 'dp', 'tensor'), may hold values from 1.981661e-10 to 7.926644e-10
Outputs:
- out_tokens: bfloat16 [32, 768, 2048], P('dp', 'tensor')
- tokens_grad: bfloat16 [32, 768, 2048], P('dp', 'tensor')
- grad_norm: float32 [], replicated
- grad_wide: float32 [7, 128, 2048], P(None, None, ('dp', 'tensor'))
- grad_attention: float32 [4, 128, 2048], P(None, 'dp', 'tensor')
- grad_feedforward: float32 [3, 128, 5632], P(None, 'dp', 'tensor')
- next_wide: float32 [7, 128, 2048], P(None, None, ('dp', 'tensor'))
- next_attention: float32 [4, 128, 2048], P(None, 'dp', 'tensor')
- next_feedforward: float32 [3, 128, 5632], P(None, 'dp', 'tensor')
- next_moment_wide: float32 [7, 128, 2048], P(None, None, ('dp', 'tensor'))
- next_moment_attention: float32 [4, 128, 2048], P(None, 'dp', 'tensor')
- next_moment_feedforward: float32 [3, 128, 5632], P(None, 'dp', 'tensor')
- next_variance_wide: float32 [7, 128, 2048], P(None, None, ('dp', 'tensor'))
- next_variance_attention: float32 [4, 128, 2048], P(None, 'dp', 'tensor')
- next_variance_feedforward: float32 [3, 128, 5632], P(None, 'dp', 'tensor')
All inputs are finite; a program needn't handle non-finite values.
Results may differ from a plain program's by a relative error of at most 0.025.
Values may be sent and summed in bfloat16 or wider, within the bound.
No kernel may reach another device: no remote copies, remote signals or barrier semaphores. Data moves between devices by JAX's collectives and lax.ppermute only.
A program may use at most 192 MiB of HBM per device.

v0:
```python
import jax
import jax.numpy as jnp
from jax import lax
from jax.sharding import PartitionSpec as P

HEAD_DIM = 128
ADAPTERS = 8
RANK = 16
BLOCK = 256
STEP = 10


NORM_EPS = 1e-05
ADAPTER_SCALING = 0.5
LAMBDA_INIT = 0.2
OUT_GAIN = 0.8
CLIP_NORM = 1.0
LEARN_RATE = 0.05
BETA_FIRST = 0.9
BETA_SECOND = 0.999
ADAM_EPS = 1e-08
WEIGHT_DECAY = 0.01
NEG_LARGE = -1e30


def product(left, right):
    return jnp.dot(left, right, preferred_element_type=jnp.float32)


def contract_matrices(form, left, right):
    return jnp.einsum(form, left, right, preferred_element_type=jnp.float32)


def choose(stacked, onehot):
    shaped = stacked.reshape(stacked.shape[0], ADAPTERS, RANK, stacked.shape[2])
    picked = jnp.einsum(
        "e,xerc->xrc", onehot.astype(jnp.bfloat16), shaped, preferred_element_type=jnp.float32
    )
    return picked.astype(jnp.bfloat16)


def spread(gradient, onehot):
    placed = onehot[None, :, None, None] * gradient[:, None, :, :]
    return placed.reshape(gradient.shape[0], ADAPTERS * RANK, gradient.shape[2])


def unpack(gathered, onehot):
    whole_inputs, whole_output, whole_hidden, whole_down, attention_stack, feedforward_stack = (
        gathered
    )
    return (
        whole_inputs,
        whole_output,
        whole_hidden,
        whole_down,
        choose(attention_stack, onehot),
        choose(feedforward_stack, onehot),
    )


def norm_forward(values, gain_value):
    factor = lax.rsqrt(jnp.mean(values * values, axis=-1, keepdims=True) + NORM_EPS)
    return (values * factor * gain_value, factor)


def norm_backward(values, factor, gain_value, gradient):
    scaled = gradient * gain_value
    return factor * (
        scaled - values * factor * factor * jnp.mean(scaled * values, axis=-1, keepdims=True)
    )


def head_scores(query_pair, key_pair, mask_bias):
    return contract_matrices("cld,cmd->clm", query_pair, key_pair) * HEAD_DIM ** (-0.5) + mask_bias


def head_forward(query_pair, key_pair, values, lambda_one, mask_bias):
    scores = head_scores(query_pair, key_pair, mask_bias)
    row_max = jnp.max(scores, axis=-1, keepdims=True)
    shifted = jnp.exp(scores - row_max)
    row_sum = jnp.sum(shifted, axis=-1, keepdims=True)
    probabilities = shifted / row_sum
    log_total = row_max + jnp.log(row_sum)
    combined = (probabilities[0] - lambda_one * probabilities[1]).astype(jnp.bfloat16)
    return (product(combined, values), log_total[..., 0])


def head_backward(query_pair, key_pair, values, lambda_one, log_total, grad_out, mask_bias):
    scores = head_scores(query_pair, key_pair, mask_bias)
    probabilities = jnp.exp(scores - log_total[..., None])
    combined = (probabilities[0] - lambda_one * probabilities[1]).astype(jnp.bfloat16)
    grad_values = contract_matrices("lm,ld->md", combined, grad_out)
    grad_combined = contract_matrices("ld,md->lm", grad_out, values)
    weighting = jnp.stack([jnp.ones_like(lambda_one), -lambda_one])
    grad_probs = weighting[:, None, None] * grad_combined[None]
    row_inner = jnp.sum(grad_probs * probabilities, axis=-1, keepdims=True)
    grad_scores = (probabilities * (grad_probs - row_inner) * HEAD_DIM ** (-0.5)).astype(
        jnp.bfloat16
    )
    grad_query = contract_matrices("clm,cmd->cld", grad_scores, key_pair)
    grad_key = contract_matrices("clm,cld->cmd", grad_scores, query_pair)
    return (grad_query, grad_key, grad_values)


def adam_step(parameter, gradient, moment, variance, factor):
    clipped = gradient * factor
    moment_new = BETA_FIRST * moment + (1.0 - BETA_FIRST) * clipped
    variance_new = BETA_SECOND * variance + (1.0 - BETA_SECOND) * clipped * clipped
    moment_hat = moment_new / (1.0 - BETA_FIRST**STEP)
    variance_hat = variance_new / (1.0 - BETA_SECOND**STEP)
    updated = parameter - LEARN_RATE * (
        moment_hat / (jnp.sqrt(variance_hat) + ADAM_EPS) + WEIGHT_DECAY * parameter
    )
    return (clipped, updated, moment_new, variance_new)


def local(
    tokens,
    cotangent,
    adapter_ids,
    norm_gains,
    lambda_vectors,
    weight_inputs,
    weight_output,
    hidden_weight_matrix,
    weight_down,
    adapter_wide,
    adapter_attention,
    adapter_feedforward,
    moment_wide,
    variance_wide,
    moment_attention,
    variance_attention,
    moment_feedforward,
    variance_feedforward,
):
    local_tokens = tokens[0].astype(jnp.float32)
    upstream_b = cotangent[0]
    onehot = (jnp.arange(ADAPTERS, dtype=jnp.int32) == adapter_ids[0]).astype(jnp.float32)
    gain_values = norm_gains.astype(jnp.float32)
    lambda_all = (
        jnp.exp(jnp.sum(lambda_vectors[0] * lambda_vectors[1], axis=-1))
        - jnp.exp(jnp.sum(lambda_vectors[2] * lambda_vectors[3], axis=-1))
        + LAMBDA_INIT
    )
    heads_local = lambda_vectors.shape[1]
    length = tokens.shape[1] * lax.axis_size("tensor")
    position = jnp.arange(length, dtype=jnp.int32) // BLOCK
    mask_bias = jnp.where(position[None, :] <= position[:, None], 0.0, NEG_LARGE).astype(
        jnp.float32
    )
    frozen_parts = (
        weight_inputs,
        weight_output,
        hidden_weight_matrix,
        weight_down,
        adapter_attention.astype(jnp.bfloat16),
        adapter_feedforward.astype(jnp.bfloat16),
    )
    gathered = (
        lax.all_gather(frozen_parts[0], "dp", axis=1, tiled=True),
        lax.all_gather(frozen_parts[1], "dp", axis=1, tiled=True),
        lax.all_gather(frozen_parts[2], "dp", axis=1, tiled=True),
        lax.all_gather(frozen_parts[3], "dp", axis=1, tiled=True),
        lax.all_gather(frozen_parts[4], "dp", axis=1, tiled=True),
        lax.all_gather(frozen_parts[5], "dp", axis=1, tiled=True),
    )
    whole_inputs, whole_output, whole_hidden, whole_down, picked_attention, selected_feedforward = (
        unpack(gathered, onehot)
    )
    wide_columns = lax.all_gather(
        adapter_wide.astype(jnp.bfloat16), ("dp", "tensor"), axis=2, tiled=True
    )
    picked_wide = choose(wide_columns, onehot)
    normed_one, scale_one = norm_forward(local_tokens, gain_values[0])
    normed_one_b = normed_one.astype(jnp.bfloat16)
    lowrank_inputs = contract_matrices("td,xrd->xtr", normed_one_b, picked_wide[0:3]).astype(
        jnp.bfloat16
    )
    seq_normed_one, seq_lowrank_inputs = (
        lax.all_gather(normed_one_b, "tensor", axis=0, tiled=True),
        lax.all_gather(lowrank_inputs, "tensor", axis=1, tiled=True),
    )
    projected = contract_matrices(
        "ld,xdc->xlc", seq_normed_one, whole_inputs
    ) + ADAPTER_SCALING * contract_matrices(
        "xlr,xrc->xlc", seq_lowrank_inputs, picked_attention[0:3]
    )
    projected_b = projected.astype(jnp.bfloat16)
    query_heads = projected_b[0].reshape(length, heads_local, 2, HEAD_DIM).transpose(1, 2, 0, 3)
    key_heads = projected_b[1].reshape(length, heads_local, 2, HEAD_DIM).transpose(1, 2, 0, 3)
    value_heads = projected_b[2].reshape(length, heads_local, 2 * HEAD_DIM).transpose(1, 0, 2)

    def forward_head(head_items):
        query_pair, key_pair, values, lambda_one = head_items
        return head_forward(query_pair, key_pair, values, lambda_one, mask_bias)

    raw_heads, log_totals = lax.map(forward_head, (query_heads, key_heads, value_heads, lambda_all))
    head_factor = lax.rsqrt(jnp.mean(raw_heads * raw_heads, axis=-1, keepdims=True) + NORM_EPS)
    attention_b = (
        (raw_heads * head_factor * OUT_GAIN)
        .transpose(1, 0, 2)
        .reshape(length, -1)
        .astype(jnp.bfloat16)
    )
    output_part = product(attention_b, whole_output)
    lowrank_out_part = contract_matrices("lc,rc->lr", attention_b, picked_attention[3])
    attention_local, lowrank_out = (
        lax.psum_scatter(
            output_part.astype(jnp.bfloat16), "tensor", scatter_dimension=0, tiled=True
        ).astype(jnp.float32),
        lax.psum_scatter(
            lowrank_out_part.astype(jnp.bfloat16), "tensor", scatter_dimension=0, tiled=True
        ).astype(jnp.float32),
    )
    lowrank_out_b = lowrank_out.astype(jnp.bfloat16)
    residual_one = (
        local_tokens + attention_local + ADAPTER_SCALING * product(lowrank_out_b, picked_wide[5])
    )
    second_normalized, scale_two = norm_forward(residual_one, gain_values[1])
    normed_two_b = second_normalized.astype(jnp.bfloat16)
    low_rank_hidden = contract_matrices("td,xrd->xtr", normed_two_b, picked_wide[3:5]).astype(
        jnp.bfloat16
    )
    seq_normed_two, sequence_low_rank_hidden = (
        lax.all_gather(normed_two_b, "tensor", axis=0, tiled=True),
        lax.all_gather(low_rank_hidden, "tensor", axis=1, tiled=True),
    )
    gate_up_product = contract_matrices(
        "ld,xdf->xlf", seq_normed_two, whole_hidden
    ) + ADAPTER_SCALING * contract_matrices(
        "dmq,dqo->dmo", sequence_low_rank_hidden, selected_feedforward[0:2]
    )
    hidden_b = (jax.nn.silu(gate_up_product[0]) * gate_up_product[1]).astype(jnp.bfloat16)
    down_part = product(hidden_b, whole_down)
    lowrank_down_part = contract_matrices("lf,rf->lr", hidden_b, selected_feedforward[2])
    down_local, lowrank_down = (
        lax.psum_scatter(
            down_part.astype(jnp.bfloat16), "tensor", scatter_dimension=0, tiled=True
        ).astype(jnp.float32),
        lax.psum_scatter(
            lowrank_down_part.astype(jnp.bfloat16), "tensor", scatter_dimension=0, tiled=True
        ).astype(jnp.float32),
    )
    lowrank_down_b = lowrank_down.astype(jnp.bfloat16)
    result = residual_one + down_local + ADAPTER_SCALING * product(lowrank_down_b, picked_wide[6])
    regathered = (
        lax.all_gather(frozen_parts[0], "dp", axis=1, tiled=True),
        lax.all_gather(frozen_parts[1], "dp", axis=1, tiled=True),
        lax.all_gather(frozen_parts[2], "dp", axis=1, tiled=True),
        lax.all_gather(frozen_parts[3], "dp", axis=1, tiled=True),
        lax.all_gather(frozen_parts[4], "dp", axis=1, tiled=True),
        lax.all_gather(frozen_parts[5], "dp", axis=1, tiled=True),
    )
    whole_inputs, whole_output, whole_hidden, whole_down, picked_attention, selected_feedforward = (
        unpack(regathered, onehot)
    )
    grad_right_down = ADAPTER_SCALING * contract_matrices("tr,td->rd", lowrank_down_b, upstream_b)
    grad_lowrank_down = (
        ADAPTER_SCALING * contract_matrices("td,rd->tr", upstream_b, picked_wide[6])
    ).astype(jnp.bfloat16)
    seq_upstream, seq_grad_lowrank_down = (
        lax.all_gather(upstream_b, "tensor", axis=0, tiled=True),
        lax.all_gather(grad_lowrank_down, "tensor", axis=0, tiled=True),
    )
    grad_hidden = contract_matrices("ld,fd->lf", seq_upstream, whole_down) + contract_matrices(
        "lr,rf->lf", seq_grad_lowrank_down, selected_feedforward[2]
    )
    grad_left_down = contract_matrices("lr,lf->rf", seq_grad_lowrank_down, hidden_b)
    sigmoid_gate = jax.nn.sigmoid(gate_up_product[0])
    grad_gate = (
        grad_hidden
        * gate_up_product[1]
        * sigmoid_gate
        * (1.0 + gate_up_product[0] * (1.0 - sigmoid_gate))
    )
    grad_upper = grad_hidden * gate_up_product[0] * sigmoid_gate
    gate_up_gradient_second = jnp.stack([grad_gate, grad_upper]).astype(jnp.bfloat16)
    right_hidden_gradient = ADAPTER_SCALING * contract_matrices(
        "tau,tan->tun", sequence_low_rank_hidden, gate_up_gradient_second
    )
    grad_lowrank_hidden_part = ADAPTER_SCALING * contract_matrices(
        "shw,sqw->shq", gate_up_gradient_second, selected_feedforward[0:2]
    )
    grad_normed_two_part = contract_matrices("xlf,xdf->ld", gate_up_gradient_second, whole_hidden)
    grad_normed_two, grad_lowrank_hidden = (
        lax.psum_scatter(
            grad_normed_two_part.astype(jnp.bfloat16), "tensor", scatter_dimension=0, tiled=True
        ).astype(jnp.float32),
        lax.psum_scatter(
            grad_lowrank_hidden_part.astype(jnp.bfloat16), "tensor", scatter_dimension=1, tiled=True
        ).astype(jnp.float32),
    )
    grad_lowrank_hidden_b = grad_lowrank_hidden.astype(jnp.bfloat16)
    grad_left_hidden = contract_matrices("xtr,td->xrd", grad_lowrank_hidden_b, normed_two_b)
    grad_normed_two = grad_normed_two + contract_matrices(
        "xtr,xrd->td", grad_lowrank_hidden_b, picked_wide[3:5]
    )
    grad_residual = upstream_b.astype(jnp.float32) + norm_backward(
        residual_one, scale_two, gain_values[1], grad_normed_two
    )
    grad_branch_b = grad_residual.astype(jnp.bfloat16)
    grad_right_out = ADAPTER_SCALING * contract_matrices("tr,td->rd", lowrank_out_b, grad_branch_b)
    grad_lowrank_out = (
        ADAPTER_SCALING * contract_matrices("td,rd->tr", grad_branch_b, picked_wide[5])
    ).astype(jnp.bfloat16)
    seq_grad_branch, seq_grad_lowrank_out = (
        lax.all_gather(grad_branch_b, "tensor", axis=0, tiled=True),
        lax.all_gather(grad_lowrank_out, "tensor", axis=0, tiled=True),
    )
    grad_attention_in = contract_matrices(
        "ld,cd->lc", seq_grad_branch, whole_output
    ) + contract_matrices("lr,rc->lc", seq_grad_lowrank_out, picked_attention[3])
    grad_left_out = contract_matrices("lr,lc->rc", seq_grad_lowrank_out, attention_b)
    grad_heads = grad_attention_in.reshape(length, heads_local, 2 * HEAD_DIM).transpose(1, 0, 2)
    grad_raw_b = norm_backward(raw_heads, head_factor, OUT_GAIN, grad_heads).astype(jnp.bfloat16)

    def backward_head(head_items):
        query_pair, key_pair, values, lambda_one, log_total, grad_out = head_items
        return head_backward(
            query_pair, key_pair, values, lambda_one, log_total, grad_out, mask_bias
        )

    grad_query, grad_key, grad_value = lax.map(
        backward_head, (query_heads, key_heads, value_heads, lambda_all, log_totals, grad_raw_b)
    )
    grad_projected_b = jnp.stack(
        [
            grad_query.transpose(2, 0, 1, 3).reshape(length, -1),
            grad_key.transpose(2, 0, 1, 3).reshape(length, -1),
            grad_value.transpose(1, 0, 2).reshape(length, -1),
        ]
    ).astype(jnp.bfloat16)
    grad_right_inputs = ADAPTER_SCALING * contract_matrices(
        "xlr,xlc->xrc", seq_lowrank_inputs, grad_projected_b
    )
    grad_lowrank_inputs_part = ADAPTER_SCALING * contract_matrices(
        "xlc,xrc->xlr", grad_projected_b, picked_attention[0:3]
    )
    grad_normed_one_part = contract_matrices("xlc,xdc->ld", grad_projected_b, whole_inputs)
    grad_normed_one, grad_lowrank_inputs = (
        lax.psum_scatter(
            grad_normed_one_part.astype(jnp.bfloat16), "tensor", scatter_dimension=0, tiled=True
        ).astype(jnp.float32),
        lax.psum_scatter(
            grad_lowrank_inputs_part.astype(jnp.bfloat16), "tensor", scatter_dimension=1, tiled=True
        ).astype(jnp.float32),
    )
    grad_lowrank_inputs_b = grad_lowrank_inputs.astype(jnp.bfloat16)
    grad_left_inputs = contract_matrices("xtr,td->xrd", grad_lowrank_inputs_b, normed_one_b)
    grad_normed_one = grad_normed_one + contract_matrices(
        "xtr,xrd->td", grad_lowrank_inputs_b, picked_wide[0:3]
    )
    grad_input = grad_residual + norm_backward(
        local_tokens, scale_one, gain_values[0], grad_normed_one
    )
    wide_picked_grads = jnp.concatenate(
        [grad_left_inputs, grad_left_hidden, grad_right_out[None], grad_right_down[None]], axis=0
    )
    attention_picked_grads = jnp.concatenate([grad_right_inputs, grad_left_out[None]], axis=0)
    feedforward_picked_grads = jnp.concatenate(
        [right_hidden_gradient, grad_left_down[None]], axis=0
    )
    grads_attention, grads_feedforward = (
        lax.psum_scatter(
            spread(attention_picked_grads, onehot).astype(jnp.bfloat16),
            "dp",
            scatter_dimension=1,
            tiled=True,
        ).astype(jnp.float32),
        lax.psum_scatter(
            spread(feedforward_picked_grads, onehot).astype(jnp.bfloat16),
            "dp",
            scatter_dimension=1,
            tiled=True,
        ).astype(jnp.float32),
    )
    grads_wide = lax.psum_scatter(
        spread(wide_picked_grads, onehot), ("dp", "tensor"), scatter_dimension=2, tiled=True
    )
    local_squares = (
        jnp.sum(grads_wide * grads_wide)
        + jnp.sum(grads_attention * grads_attention)
        + jnp.sum(grads_feedforward * grads_feedforward)
    )
    total_squares = lax.psum(local_squares, ("dp", "tensor"))
    grad_norm = jnp.sqrt(total_squares)
    factor = CLIP_NORM / (grad_norm + 1e-06)
    wide_new = adam_step(adapter_wide, grads_wide, moment_wide, variance_wide, factor)
    attention_new = adam_step(
        adapter_attention, grads_attention, moment_attention, variance_attention, factor
    )
    feedforward_new = adam_step(
        adapter_feedforward, grads_feedforward, moment_feedforward, variance_feedforward, factor
    )
    return (
        result.astype(jnp.bfloat16)[None],
        grad_input.astype(jnp.bfloat16)[None],
        grad_norm,
        wide_new[0],
        attention_new[0],
        feedforward_new[0],
        wide_new[1],
        attention_new[1],
        feedforward_new[1],
        wide_new[2],
        attention_new[2],
        feedforward_new[2],
        wide_new[3],
        attention_new[3],
        feedforward_new[3],
    )


def solution(mesh):
    return jax.shard_map(
        local,
        mesh=mesh,
        in_specs=(
            P("dp", "tensor", None),
            P("dp", "tensor", None),
            P("dp"),
            P(),
            P(None, "tensor", None),
            P(None, "dp", "tensor"),
            P("tensor", "dp"),
            P(None, "dp", "tensor"),
            P("tensor", "dp"),
            P(None, None, ("dp", "tensor")),
            P(None, "dp", "tensor"),
            P(None, "dp", "tensor"),
            P(None, None, ("dp", "tensor")),
            P(None, None, ("dp", "tensor")),
            P(None, "dp", "tensor"),
            P(None, "dp", "tensor"),
            P(None, "dp", "tensor"),
            P(None, "dp", "tensor"),
        ),
        out_specs=(
            P("dp", "tensor", None),
            P("dp", "tensor", None),
            P(),
            P(None, None, ("dp", "tensor")),
            P(None, "dp", "tensor"),
            P(None, "dp", "tensor"),
            P(None, None, ("dp", "tensor")),
            P(None, "dp", "tensor"),
            P(None, "dp", "tensor"),
            P(None, None, ("dp", "tensor")),
            P(None, "dp", "tensor"),
            P(None, "dp", "tensor"),
            P(None, None, ("dp", "tensor")),
            P(None, "dp", "tensor"),
            P(None, "dp", "tensor"),
        ),
        check_vma=False,
    )
```

profile of v0, /device:TPU:1, one launch (start us, length us, event | category | flops | bytes accessed | tf_op | source)
XLA Modules:
  0.0 2689.9 jit_solution(13953021260231776251)
XLA Ops:
  15.3 73.8 %all_gather.55 = bf16[4,128,512]{2,0,1:T(4,128)(2,1)S(1)} all-gather(bf16[4,4,512]{2,0,1:T(4,128)(2,1)S(1)} %copy.178), channel_id=1, replica_groups=mesh['dp'=32,'tensor'=4] {'dp'}, dimensions={1}, use_global_device_ids=true | all-gather | bytes 540672 | tf_op jit(solution)/shard_map/all_gather | solution.py:165
  90.0 128.6 %all-gather.18.cloned.1.call-done = bf16[7,128,2048]{1,2,0:T(8,128)(2,1)} async-done(((bf16[7,128,16]{1,2,0:T(8,128)(2,1)}), bf16[7,128,2048]{1,2,0:T(8,128)(2,1)}) %all-gather.18.cloned.1.call-update) | async-done | bytes 3670032 | tf_op jit(solution)/shard_map/all_gather | solution.py:171
  231.2 15.1 all_gather.54
  256.2 157.4 %all-gather.16.cloned.1.call-done = bf16[3,2048,512]{2,1,0:T(8,128)(2,1)} async-done(((bf16[3,64,512]{2,1,0:T(8,128)(2,1)}), bf16[3,2048,512]{2,1,0:T(8,128)(2,1)}) %all-gather.16.cloned.1.call-update) | async-done | bytes 6291472 | tf_op jit(solution)/shard_map/all_gather | solution.py:161
  443.1 123.8 %all-gather.20.cloned.1.call-done = bf16[512,2048]{0,1:T(8,128)(2,1)} async-done(((bf16[512,64]{0,1:T(8,128)(2,1)}), bf16[512,2048]{0,1:T(8,128)(2,1)}) %all-gather.20.cloned.1.call-update) | async-done | bytes 2097168 | tf_op jit(solution)/shard_map/all_gather | solution.py:162
  576.3 40.2 %reduce-scatter.30.cloned.1.call-done = bf16[192,16]{1,0:T(8,128)(2,1)} async-done(((bf16[768,16]{1,0:T(8,128)(2,1)}), bf16[192,16]{1,0:T(8,128)(2,1)}) %reduce-scatter.30.cloned.1.call-update) | async-done | bytes 6160
  616.5 47.0 %reduce-scatter.20.cloned.1.call-done = bf16[192,2048]{1,0:T(8,128)(2,1)} async-done(((bf16[768,2048]{1,0:T(8,128)(2,1)}), bf16[192,2048]{1,0:T(8,128)(2,1)}) %reduce-scatter.20.cloned.1.call-update) | async-done | bytes 786448 | tf_op jit(solution)/shard_map/reduce_scatter | solution.py:209
  666.8 131.2 %all-gather.26.cloned.1.call-done = bf16[3,128,1408]{2,0,1:T(4,128)(2,1)} async-done(((bf16[3,4,1408]{2,0,1:T(4,128)(2,1)}), bf16[3,128,1408]{2,0,1:T(4,128)(2,1)}) %all-gather.26.cloned.1.call-update) | async-done | bytes 1081360 | tf_op jit(solution)/shard_map/all_gather | solution.py:166
  802.9 27.5 %all-gather.1 = bf16[4,192,16]{1,2,0:T(8,128)(2,1)S(1)} all-gather(bf16[1,192,16]{1,2,0:T(8,128)(2,1)S(1)} %fusion.129), channel_id=1, replica_groups=mesh['dp'=32,'tensor'=4] {'tensor'}, dimensions={0}, use_global_device_ids=true | all-gather | bytes 30720 | tf_op jit(solution)/shard_map/all_gather | solution.py:264
  831.1 22.2 all-gather.32.cloned.1.call-done
  853.3 154.8 %all-gather.28.cloned.1.call-done = bf16[1408,2048]{0,1:T(8,128)(2,1)} async-done(((bf16[1408,64]{0,1:T(8,128)(2,1)}), bf16[1408,2048]{0,1:T(8,128)(2,1)}) %all-gather.28.cloned.1.call-update) | async-done | bytes 5767184 | tf_op jit(solution)/shard_map/all_gather | solution.py:164
  1019.9 29.0 %all_gather.59 = bf16[2,768,16]{2,0,1:T(2,128)(2,1)S(1)} all-gather(bf16[2,192,16]{2,0,1:T(2,128)(2,1)} %copy.109), channel_id=1, replica_groups=mesh['dp'=32,'tensor'=4] {'tensor'}, dimensions={1}, use_global_device_ids=true | all-gather | bytes 61440 | tf_op jit(solution)/shard_map/all_gather | solution.py:227
  1049.9 233.0 %all-gather.24.cloned.1.call-done = bf16[2,2048,1408]{2,1,0:T(8,128)(2,1)} async-done(((bf16[2,64,1408]{2,1,0:T(8,128)(2,1)}), bf16[2,2048,1408]{2,1,0:T(8,128)(2,1)}) %all-gather.24.cloned.1.call-update) | async-done | bytes 11534352 | tf_op jit(solution)/shard_map/all_gather | solution.py:163
  1282.9 31.9 %all-gather.22.cloned.1.call-done = bf16[768,2048]{1,0:T(8,128)(2,1)} async-done(((bf16[192,2048]{1,0:T(8,128)(2,1)}), bf16[768,2048]{1,0:T(8,128)(2,1)}) %all-gather.22.cloned.1.call-update) | async-done | bytes 3145744 | tf_op jit(solution)/shard_map/all_gather | solution.py:226
  1314.8 13.7 fusion.88
  1343.8 14.4 bitcast_convert_fusion.1
  1370.3 46.3 %reduce-scatter.24.cloned.1.call-done = bf16[192,2048]{1,0:T(8,128)(2,1)} async-done(((bf16[768,2048]{1,0:T(8,128)(2,1)}), bf16[192,2048]{1,0:T(8,128)(2,1)}) %reduce-scatter.24.cloned.1.call-update) | async-done | bytes 786448 | tf_op jit(solution)/shard_map/reduce_scatter | solution.py:287
  1436.3 17.3 all-gather.30.cloned.1.call-done
  1459.9 45.0 %while.31 = (s32[]{:T(128)}, bf16[2,2,768,128]{3,2,1,0:T(8,128)(2,1)}, bf16[2,2,768,128]{3,2,1,0:T(8,128)(2,1)}, bf16[2,768,256]{2,1,0:T(8,128)(2,1)}, bf16[2,2,...) while((s32[]{:T(128)}, ...), condition=%wide.region_19.20_spmd.clone.clone, body=%wide.region_17.19_spmd.clone.sunk.clone | while | flops 1532957184 | bytes 62550796 | solution.py:324
  1570.6 25.5 reduce-scatter.22.cloned.1.call-done
  1598.5 289.3 %all-reduce.5.cloned.1.call-done = (bf16[4,128,512]{2,1,0:T(8,128)(2,1)}, bf16[3,128,1408]{2,1,0:T(8,128)(2,1)}) async-done(((bf16[4,128,512]{2,1,0:T(8,128)(2,1)}, bf16[3,128,1408]{2,1,0:T(8,128)(2,1)}), (bf16[4,128,512]{2,1,0:T(8,128)(2,1)}, bf16[3,128,1408]{2,1,0:T(8,128)(2,1)})) %all-reduce.5.cloned.1.call-update) | async-done | bytes 1605648
  1890.6 61.4 %reduce-scatter.26.cloned.1.call-done = bf16[192,2048]{1,0:T(8,128)(2,1)} async-done(((bf16[768,2048]{1,0:T(8,128)(2,1)}), bf16[192,2048]{1,0:T(8,128)(2,1)}) %reduce-scatter.26.cloned.1.call-update) | async-done | bytes 786448 | tf_op jit(solution)/shard_map/reduce_scatter | solution.py:342
  1955.5 642.1 %reduce-scatter.28.cloned.1.call-done = f32[7,128,16]{1,0,2:T(8,128)} async-done(((f32[7,128,2048]{1,0,2:T(8,128)}), f32[7,128,16]{1,0,2:T(8,128)}) %reduce-scatter.28.cloned.1.call-update) | async-done | bytes 57360 | tf_op jit(solution)/shard_map/reduce_scatter | solution.py:378
  2604.8 69.2 %psum.7 = f32[]{:T(128)} all-reduce(f32[]{:T(128)S(6)} %add.222), channel_id=1, replica_groups=mesh['dp'=32,'tensor'=4] {'dp','tensor'}, use_global_device_ids=true, to_apply=%region_29.30 | all-reduce | flops 1 | bytes 8 | tf_op jit(solution)/shard_map/psum | solution.py:386
  (339 shorter events, 284.0 us)
Async XLA Ops:
  7.2 211.5 %all-gather.18.cloned.1.call-start = ((), (), s32[]{:S(2)}) async-start(), calls=%async_computation.11 | async-start | bytes 3698688 | tf_op jit(solution)/shard_map/all_gather | solution.py:171
  8.7 247.5 %all-gather.14.cloned.1.call-start = ((), (), s32[]{:S(2)}) async-start(), calls=%async_computation.9 | async-start | bytes 3932160 | tf_op jit(solution)/shard_map/all_gather | solution.py:181
  13.2 400.4 %all-gather.16.cloned.1.call-start = ((), (), s32[]{:S(2)}) async-start(), calls=%async_computation.10 | async-start | bytes 6488064 | tf_op jit(solution)/shard_map/all_gather | solution.py:161
  14.0 552.9 %all-gather.20.cloned.1.call-start = ((), (), s32[]{:S(2)}) async-start(), calls=%async_computation.12 | async-start | bytes 2162688 | tf_op jit(solution)/shard_map/all_gather | solution.py:162
  14.6 601.9 %reduce-scatter.30.cloned.1.call-start = ((), (), s32[]{:S(2)}) async-start(), calls=%async_computation.24 | async-start | bytes 245760
  443.0 220.4 %reduce-scatter.20.cloned.1.call-start = ((), (), s32[]{:S(2)}) async-start(), calls=%async_computation.13 | async-start | bytes 3932160 | tf_op jit(solution)/shard_map/reduce_scatter | solution.py:209
  572.2 225.8 %all-gather.26.cloned.1.call-start = ((), (), s32[]{:S(2)}) async-start(), calls=%async_computation.16 | async-start | bytes 1486848 | tf_op jit(solution)/shard_map/all_gather | solution.py:166
  573.8 279.5 %all-gather.32.cloned.1.call-start = ((), (), s32[]{:S(2)}) async-start(), calls=%async_computation.23 | async-start | bytes 3932160 | tf_op jit(solution)/shard_map/all_gather | solution.py:263
  574.5 433.6 %all-gather.28.cloned.1.call-start = ((), (), s32[]{:S(2)}) async-start(), calls=%async_computation.17 | async-start | bytes 5947392 | tf_op jit(solution)/shard_map/all_gather | solution.py:164
  575.3 707.6 %all-gather.24.cloned.1.call-start = ((), (), s32[]{:S(2)}) async-start(), calls=%async_computation.15 | async-start | bytes 11894784 | tf_op jit(solution)/shard_map/all_gather | solution.py:163
  575.8 739.0 %all-gather.22.cloned.1.call-start = ((), (), s32[]{:S(2)}) async-start(), calls=%async_computation.14 | async-start | bytes 3932160 | tf_op jit(solution)/shard_map/all_gather | solution.py:226
  665.4 753.1 %copy-start = (f32[192,2048]{1,0:T(8,128)}, f32[192,2048]{1,0:T(8,128)S(1)}, u32[]{:S(2)}) copy-start(f32[192,2048]{1,0:T(8,128)S(1)} %get-tuple-element.309) | copy-start | bytes 4718596
  666.8 702.5 %reduce-scatter.34.cloned.1.call-start = ((), (), s32[]{:S(2)}) async-start(), calls=%async_computation.26 | async-start | bytes 245760
  1343.6 73.0 %reduce-scatter.24.cloned.1.call-start = ((), (), s32[]{:S(2)}) async-start(), calls=%async_computation.19 | async-start | bytes 3932160 | tf_op jit(solution)/shard_map/reduce_scatter | solution.py:287
  1358.3 95.3 %all-gather.30.cloned.1.call-start = ((), (), s32[]{:S(2)}) async-start(), calls=%async_computation.20 | async-start | bytes 3932160 | tf_op jit(solution)/shard_map/all_gather | solution.py:308
  1421.0 129.7 %reduce-scatter.32.cloned.1.call-start = ((), (), s32[]{:S(2)}) async-start(), calls=%async_computation.25 | async-start | bytes 245760
  1427.7 126.3 %reduce-scatter.36.cloned.1.call-start = ((), (), s32[]{:S(2)}) async-start(), calls=%async_computation.27 | async-start | bytes 245760
  1523.3 72.7 %reduce-scatter.22.cloned.1.call-start = ((), (), s32[]{:S(2)}) async-start(), calls=%async_computation.18 | async-start | bytes 3932160 | tf_op jit(solution)/shard_map/reduce_scatter | solution.py:238
  1532.4 355.3 %all-reduce.5.cloned.1.call-start = ((), (), s32[]{:S(2)}) async-start(), calls=%async_computation.28 | async-start | bytes 3211264
  1541.2 410.9 %reduce-scatter.26.cloned.1.call-start = ((), (), s32[]{:S(2)}) async-start(), calls=%async_computation.21 | async-start | bytes 3932160 | tf_op jit(solution)/shard_map/reduce_scatter | solution.py:342
  1550.6 1047.0 %reduce-scatter.28.cloned.1.call-start = ((), (), s32[]{:S(2)}) async-start(), calls=%async_computation.22 | async-start | bytes 8454144 | tf_op jit(solution)/shard_map/reduce_scatter | solution.py:378
  1598.5 1002.5 %copy-start.55 = (f32[192]{0:T(256)S(1)}, f32[192]{0:T(256)}, u32[]{:S(2)}) copy-start(f32[192]{0:T(256)} %copy-done.53) | copy-start | bytes 2308
  1598.5 1002.5 %copy-start.57 = (f32[192]{0:T(256)S(1)}, f32[192]{0:T(256)}, u32[]{:S(2)}) copy-start(f32[192]{0:T(256)} %copy-done.56) | copy-start | bytes 2308
  1598.5 1002.5 %copy-start.59 = (f32[192]{0:T(256)S(1)}, f32[192]{0:T(256)}, u32[]{:S(2)}) copy-start(f32[192]{0:T(256)} %copy-done.58) | copy-start | bytes 2308
  (68 other events, 4006.7 us)
Sparse Core Ops, SparseCore 0:
  10.2 208.3 all-gather.17
  220.9 35.3 all-gather.13
  257.9 155.6 all-gather.15
  415.1 151.6 all-gather.19
  569.3 47.1 reduce-scatter.29
  618.9 44.4 reduce-scatter.19
  665.7 132.2 all-gather.25
  799.8 53.4 all-gather.31
  855.1 153.0 all-gather.27
  1009.7 273.1 all-gather.23
  1284.7 30.1 all-gather.21
  1343.7 25.5 reduce-scatter.33
  1372.1 44.4 reduce-scatter.23
  1421.1 32.4 all-gather.29
  1456.0 25.5 reduce-scatter.31
  1523.5 25.6 reduce-scatter.35
  1551.6 44.4 reduce-scatter.21
  1598.7 289.0 all-reduce.4
  1890.4 61.6 reduce-scatter.25
  1954.4 643.1 reduce-scatter.27
where the time goes:
time: 2700 us; the launch traced here: 2690 us
  waiting for transfers between devices  2180 us (81%)
  blocking collectives  222 us (8%)
  matrix products  170 us (6%)
  local copies, waits for them, and re-layouts  62.4 us (2%)
  other arithmetic  36.3 us (1%)
    reduce_scatter x1, waiting for transfers between devices, local(): lax.psum_scatter(spread(wide_picked_grads, onehot), ('dp', 'tensor'), sca...  642 us
    unnamed x25, waiting for transfers between devices  344 us
    all_gather x1, waiting for transfers between devices, local(): lax.all_gather(frozen_parts[2], 'dp', axis=1, tiled=True)  233 us
    all_gather x1, waiting for transfers between devices, local(): lax.all_gather(frozen_parts[0], 'dp', axis=1, tiled=True)  157 us
    all_gather x1, waiting for transfers between devices, local(): lax.all_gather(frozen_parts[3], 'dp', axis=1, tiled=True)  155 us
    dot_general x40, matrix products, contract_matrices(): return jnp.einsum(form, left, right, preferred_element_type=jnp.float32)  139 us
    all_gather x1, waiting for transfers between devices, local(): lax.all_gather(frozen_parts[5], 'dp', axis=1, tiled=True)  131 us
    all_gather x1, waiting for transfers between devices, local(): lax.all_gather(adapter_wide.astype(jnp.bfloat16), ('dp', 'tensor'), axis=...  129 us
  transfers between devices with their start and end apart: 20, of which 18 were waited for; matrix products, arithmetic and copies ran while one was open for 8% of the time, Pallas kernels for 0%

commit v1 on v0

v1 whole, which is shorter than its diff:
```python
import jax
import jax.numpy as jnp
from jax import lax
from jax.sharding import PartitionSpec as P

HEAD_DIM = 128
ADAPTERS = 8
RANK = 16
BLOCK = 256
STEP = 10


NORM_EPS = 1e-05
ADAPTER_SCALING = 0.5
LAMBDA_INIT = 0.2
OUT_GAIN = 0.8
CLIP_NORM = 1.0
LEARN_RATE = 0.05
BETA_FIRST = 0.9
BETA_SECOND = 0.999
ADAM_EPS = 1e-08
WEIGHT_DECAY = 0.01
NEG_LARGE = -1e30
AXES = ("dp", "tensor")
B16 = jnp.bfloat16
F32 = jnp.float32


def product(left, right):
    return jnp.dot(left, right, preferred_element_type=F32)


def contract(form, left, right):
    return jnp.einsum(form, left, right, preferred_element_type=F32)


def index_of(z, y, x, core):
    x, y, z, core = x % 4, y % 4, z % 4, core % 2
    return ((z * 4 + y) * 2 + x % 2) * 4 + (x // 2) * 2 + core


def routes(move):
    pairs = []
    for z in range(4):
        for y in range(4):
            for x in range(4):
                for core in range(2):
                    pairs.append((index_of(z, y, x, core), index_of(*move(z, y, x, core))))
    return pairs


UP_Z = routes(lambda z, y, x, c: (z + 1, y, x, c))
DOWN_Z = routes(lambda z, y, x, c: (z - 1, y, x, c))
FAR_Z = routes(lambda z, y, x, c: (z + 2, y, x, c))
UP_Y = routes(lambda z, y, x, c: (z, y + 1, x, c))
DOWN_Y = routes(lambda z, y, x, c: (z, y - 1, x, c))
FAR_Y = routes(lambda z, y, x, c: (z, y + 2, x, c))
PAIR_X = routes(lambda z, y, x, c: (z, y, x ^ 1, c))
FAR_X = routes(lambda z, y, x, c: (z, y, x + 2, c))
CORES = routes(lambda z, y, x, c: (z, y, x, 1 - c))


def send(values, pairs):
    return lax.ppermute(values, AXES, pairs)


def put(buffer, values, *starts):
    return lax.dynamic_update_slice(buffer, values, starts)


class Place:
    def __init__(self):
        dp, tensor = lax.axis_index("dp"), lax.axis_index("tensor")
        self.z, self.y, self.x = dp // 8, (dp // 2) % 4, dp % 2
        self.far, self.core = tensor // 2, tensor % 2
        self.dp, self.tensor = dp, tensor


def gather_rows(shard, place, widths):
    z, y, x = place.z, place.y, place.x
    other = send(shard, PAIR_X)
    pair = jnp.where(x == 0, jnp.stack([shard, other]), jnp.stack([other, shard]))
    half = shard.shape[0] // 2
    full = shard.shape[1]

    def ring(block, step_up, step_down, step_far, here):
        wide = jnp.zeros((4,) + block.shape, block.dtype)
        wide = put(wide, block[None], here, 0, 0, 0)
        wide = put(wide, send(block, step_up)[None], (here + 3) % 4, 0, 0, 0)
        wide = put(wide, send(block, step_down)[None], (here + 1) % 4, 0, 0, 0)
        return put(wide, send(block, step_far)[None], (here + 2) % 4, 0, 0, 0)

    def ring_relay(plane, step_up, step_down):
        below = send(plane, step_up)
        above = send(plane, step_down)
        return (plane, below, above, send(below[:2], step_up), send(above[2:], step_down))

    part_a, part_b = pair[:, :half], pair[:, half:]
    pieces_a = ring_relay(ring(part_a, UP_Y, DOWN_Y, FAR_Y, y), UP_Z, DOWN_Z)
    pieces_b = ring_relay(ring(part_b, UP_Z, DOWN_Z, FAR_Z, z), UP_Y, DOWN_Y)
    out, start = [], 0
    for width in widths:
        whole = jnp.zeros((4, 4, 2, 2, half, width), shard.dtype)
        cut = lambda v: v[..., start : start + width]
        here, below, above, far_a, far_b = [cut(v) for v in pieces_a]
        for piece, at_z, at_y in (
            (here, z, 0),
            (below, (z + 3) % 4, 0),
            (above, (z + 1) % 4, 0),
            (far_a, (z + 2) % 4, 0),
            (far_b, (z + 2) % 4, 2),
        ):
            whole = put(whole, piece[None, :, :, None], at_z, at_y, 0, 0, 0, 0)
        here, below, above, far_a, far_b = [cut(v) for v in pieces_b]
        for piece, at_y, at_z in (
            (here, y, 0),
            (below, (y + 3) % 4, 0),
            (above, (y + 1) % 4, 0),
            (far_a, (y + 2) % 4, 0),
            (far_b, (y + 2) % 4, 2),
        ):
            whole = put(whole, piece[:, None, :, None], at_z, at_y, 0, 1, 0, 0)
        out.append(whole.reshape(64 * half, width))
        start += width
    return out


def gather_tokens(shard, place):
    core = send(shard, CORES)
    far = send(shard, FAR_X)
    far_core = send(far, CORES)
    t = place.tensor
    whole = jnp.zeros((4,) + shard.shape, shard.dtype)
    zeros = (0,) * shard.ndim
    whole = put(whole, shard[None], t, *zeros)
    whole = put(whole, core[None], t ^ 1, *zeros)
    whole = put(whole, far[None], t ^ 2, *zeros)
    whole = put(whole, far_core[None], t ^ 3, *zeros)
    return whole.reshape((4 * shard.shape[0],) + shard.shape[1:])


def scatter_tokens(partial, place):
    rows = partial.shape[0] // 4
    blocks = partial.reshape(2, 2, rows, partial.shape[1])
    away = lax.dynamic_index_in_dim(blocks, 1 - place.core, 1, keepdims=False)
    near = lax.dynamic_index_in_dim(blocks, place.core, 1, keepdims=False)
    summed = near.astype(F32) + send(away.astype(B16), CORES).astype(F32)
    leaving = lax.dynamic_index_in_dim(summed, 1 - place.far, 0, keepdims=False)
    staying = lax.dynamic_index_in_dim(summed, place.far, 0, keepdims=False)
    return staying + send(leaving.astype(B16), FAR_X).astype(F32)


def norm_forward(values, gain_value):
    factor = lax.rsqrt(jnp.mean(values * values, axis=-1, keepdims=True) + NORM_EPS)
    return (values * factor * gain_value, factor)


def norm_backward(values, factor, gain_value, gradient):
    scaled = gradient * gain_value
    return factor * (
        scaled - values * factor * factor * jnp.mean(scaled * values, axis=-1, keepdims=True)
    )


def head_scores(query_pair, key_pair, mask_bias):
    return contract("cld,cmd->clm", query_pair, key_pair) * HEAD_DIM ** (-0.5) + mask_bias


def head_forward(query_pair, key_pair, values, lambda_one, mask_bias):
    scores = head_scores(query_pair, key_pair, mask_bias)
    row_max = jnp.max(scores, axis=-1, keepdims=True)
    shifted = jnp.exp(scores - row_max)
    row_sum = jnp.sum(shifted, axis=-1, keepdims=True)
    probabilities = shifted / row_sum
    log_total = row_max + jnp.log(row_sum)
    combined = (probabilities[0] - lambda_one * probabilities[1]).astype(B16)
    return (product(combined, values), log_total[..., 0])


def head_backward(query_pair, key_pair, values, lambda_one, log_total, grad_out, mask_bias):
    scores = head_scores(query_pair, key_pair, mask_bias)
    probabilities = jnp.exp(scores - log_total[..., None])
    combined = (probabilities[0] - lambda_one * probabilities[1]).astype(B16)
    grad_values = contract("lm,ld->md", combined, grad_out)
    grad_combined = contract("ld,md->lm", grad_out, values)
    weighting = jnp.stack([jnp.ones_like(lambda_one), -lambda_one])
    grad_probs = weighting[:, None, None] * grad_combined[None]
    row_inner = jnp.sum(grad_probs * probabilities, axis=-1, keepdims=True)
    grad_scores = (probabilities * (grad_probs - row_inner) * HEAD_DIM ** (-0.5)).astype(B16)
    grad_query = contract("clm,cmd->cld", grad_scores, key_pair)
    grad_key = contract("clm,cld->cmd", grad_scores, query_pair)
    return (grad_query, grad_key, grad_values)


def adam_step(parameter, gradient, moment, variance, factor):
    clipped = gradient * factor
    moment_new = BETA_FIRST * moment + (1.0 - BETA_FIRST) * clipped
    variance_new = BETA_SECOND * variance + (1.0 - BETA_SECOND) * clipped * clipped
    moment_hat = moment_new / (1.0 - BETA_FIRST**STEP)
    variance_hat = variance_new / (1.0 - BETA_SECOND**STEP)
    updated = parameter - LEARN_RATE * (
        moment_hat / (jnp.sqrt(variance_hat) + ADAM_EPS) + WEIGHT_DECAY * parameter
    )
    return (clipped, updated, moment_new, variance_new)


def flat_rows(stacked):
    moved = stacked.astype(B16).transpose(1, 0, 2)
    return moved.reshape(stacked.shape[1], -1)


def fold_rows(rows, lanes):
    padded = jnp.pad(rows, ((0, 0), (0, 16 * lanes - rows.shape[1])))
    return padded.reshape(64, lanes)


def pick_rows(gathered, adapter, width):
    lanes = gathered.shape[1]
    mine = lax.dynamic_slice_in_dim(gathered, adapter * 256, 256, 0)
    return mine.reshape(16, 16 * lanes)[:, :width]


def local(
    tokens,
    cotangent,
    adapter_ids,
    norm_gains,
    lambda_vectors,
    weight_inputs,
    weight_output,
    hidden_weight_matrix,
    weight_down,
    adapter_wide,
    adapter_attention,
    adapter_feedforward,
    moment_wide,
    variance_wide,
    moment_attention,
    variance_attention,
    moment_feedforward,
    variance_feedforward,
):
    place = Place()
    adapter = adapter_ids[0]
    local_tokens = tokens[0].astype(F32)
    upstream_b = cotangent[0]
    gain_values = norm_gains.astype(F32)
    lambda_all = (
        jnp.exp(jnp.sum(lambda_vectors[0] * lambda_vectors[1], axis=-1))
        - jnp.exp(jnp.sum(lambda_vectors[2] * lambda_vectors[3], axis=-1))
        + LAMBDA_INIT
    )
    heads_local = lambda_vectors.shape[1]
    proj = weight_inputs.shape[2]
    ff = hidden_weight_matrix.shape[2]
    length = tokens.shape[1] * 4
    position = jnp.arange(length, dtype=jnp.int32) // BLOCK
    mask_bias = jnp.where(position[None, :] <= position[:, None], 0.0, NEG_LARGE).astype(F32)

    wide_flat = jnp.pad(
        adapter_wide.astype(B16).transpose(0, 2, 1).reshape(112, 128), ((0, 16), (0, 0))
    )
    shard_one = jnp.concatenate(
        [
            weight_inputs[0],
            weight_inputs[1],
            weight_inputs[2],
            weight_output.T,
            fold_rows(flat_rows(adapter_attention), 128),
            wide_flat[:64],
            wide_flat[64:],
        ],
        axis=1,
    )
    shard_two = jnp.concatenate(
        [
            hidden_weight_matrix[0],
            hidden_weight_matrix[1],
            fold_rows(flat_rows(adapter_feedforward[0:2]), 256),
        ],
        axis=1,
    )
    shard_three = jnp.concatenate(
        [weight_down.T, fold_rows(flat_rows(adapter_feedforward[2:3]), 128)], axis=1
    )
    w_in, w_out, fold_attention, fold_wide = gather_rows(
        shard_one, place, (3 * proj, proj, 128, 256)
    )
    w_hidden, fold_hidden = gather_rows(shard_two, place, (2 * ff, 256))
    w_down, fold_down = gather_rows(shard_three, place, (ff, 128))
    pick_attention = pick_rows(fold_attention, adapter, 4 * proj)
    pick_hidden = pick_rows(fold_hidden, adapter, 2 * ff)
    pick_down = pick_rows(fold_down, adapter, ff)

    onehot_rows = (
        jnp.arange(128)[None, :, None]
        == (adapter * RANK + jnp.arange(128) - RANK * jnp.arange(8)[:, None])[:, None, :]
    ) & (jnp.arange(128)[None, None, :] // RANK == jnp.arange(8)[:, None, None])
    wide_mine = (
        fold_wide.reshape(32, 4, 16, 2, 128).transpose(0, 2, 3, 1, 4).reshape(512, 1024)
    )
    picked_t = product(wide_mine, onehot_rows.astype(B16).reshape(1024, 128)).astype(B16)
    picked_all = gather_tokens(picked_t, place).reshape(4, 32, 16, 128)
    picked_wide = picked_all.transpose(1, 0, 2, 3).reshape(2048, 128)

    def diagonal(rows, width):
        count = rows.shape[1] // width
        column = jnp.arange(rows.shape[1]) // width
        row = jnp.arange(count * RANK) // RANK
        tiled = jnp.concatenate([rows] * count, axis=0)
        return jnp.where(row[:, None] == column[None, :], tiled, 0).astype(B16)

    half = jnp.asarray(ADAPTER_SCALING, B16)

    normed_one, scale_one = norm_forward(local_tokens, gain_values[0])
    normed_one_b = normed_one.astype(B16)
    seq_normed_one = gather_tokens(normed_one_b, place)
    seq_upstream = gather_tokens(upstream_b, place)
    lowrank_inputs = product(seq_normed_one, picked_wide).astype(B16)[:, 0:48]
    diag_in = diagonal(pick_attention[:, : 3 * proj], proj)
    projected_b = (
        product(seq_normed_one, w_in) + product(lowrank_inputs * half, diag_in)
    ).astype(B16)
    split = lambda v: v.reshape(length, heads_local, 2, HEAD_DIM).transpose(1, 2, 0, 3)
    query_heads = split(projected_b[:, :proj])
    key_heads = split(projected_b[:, proj : 2 * proj])
    value_heads = (
        projected_b[:, 2 * proj :].reshape(length, heads_local, 2 * HEAD_DIM).transpose(1, 0, 2)
    )

    def forward_head(head_items):
        query_pair, key_pair, values, lambda_one = head_items
        return head_forward(query_pair, key_pair, values, lambda_one, mask_bias)

    raw_heads, log_totals = lax.map(forward_head, (query_heads, key_heads, value_heads, lambda_all))
    head_factor = lax.rsqrt(jnp.mean(raw_heads * raw_heads, axis=-1, keepdims=True) + NORM_EPS)
    attention_b = (
        (raw_heads * head_factor * OUT_GAIN).transpose(1, 0, 2).reshape(length, -1).astype(B16)
    )
    pick_out = pick_attention[:, 3 * proj :]
    pad_rank = lambda v: jnp.pad(v, ((0, 0), (0, 128 - v.shape[1])))
    out_sum = scatter_tokens(
        jnp.concatenate(
            [
                contract("lc,dc->ld", attention_b, w_out).astype(B16),
                pad_rank(contract("lc,rc->lr", attention_b, pick_out).astype(B16)),
            ],
            axis=1,
        ),
        place,
    )
    lowrank_out_b = out_sum[:, 2048 : 2048 + RANK].astype(B16)
    residual_one = (
        local_tokens
        + out_sum[:, :2048]
        + contract("tr,dr->td", lowrank_out_b * half, picked_wide[:, 80:96])
    )

    second_normalized, scale_two = norm_forward(residual_one, gain_values[1])
    normed_two_b = second_normalized.astype(B16)
    seq_normed_two = gather_tokens(normed_two_b, place)
    lowrank_hidden = product(seq_normed_two, picked_wide).astype(B16)[:, 48:80]
    diag_hidden = diagonal(pick_hidden, ff)
    gate_up = product(seq_normed_two, w_hidden) + product(lowrank_hidden * half, diag_hidden)
    gate, upper = gate_up[:, :ff], gate_up[:, ff:]
    hidden_b = (jax.nn.silu(gate) * upper).astype(B16)
    down_sum = scatter_tokens(
        jnp.concatenate(
            [
                contract("lf,df->ld", hidden_b, w_down).astype(B16),
                pad_rank(contract("lf,rf->lr", hidden_b, pick_down).astype(B16)),
            ],
            axis=1,
        ),
        place,
    )
    lowrank_down_b = down_sum[:, 2048 : 2048 + RANK].astype(B16)
    result = (
        residual_one
        + down_sum[:, :2048]
        + contract("tr,dr->td", lowrank_down_b * half, picked_wide[:, 96:112])
    )

    grad_right_down = ADAPTER_SCALING * contract("td,tr->dr", upstream_b, lowrank_down_b)
    grad_lowrank_down = (ADAPTER_SCALING * product(seq_upstream, picked_wide)).astype(B16)[:, 96:112]
    grad_hidden = product(seq_upstream, w_down) + product(grad_lowrank_down, pick_down)
    grad_left_down = contract("lr,lf->rf", grad_lowrank_down, hidden_b)
    sigmoid_gate = jax.nn.sigmoid(gate)
    grad_gate = grad_hidden * upper * sigmoid_gate * (1.0 + gate * (1.0 - sigmoid_gate))
    grad_upper = grad_hidden * gate * sigmoid_gate
    grad_gate_up = jnp.concatenate([grad_gate.astype(B16), grad_upper.astype(B16)], axis=1)
    right_hidden = [
        ADAPTER_SCALING
        * contract(
            "lr,lf->rf",
            lowrank_hidden[:, RANK * i : RANK * (i + 1)],
            grad_gate_up[:, ff * i : ff * (i + 1)],
        )
        for i in range(2)
    ]
    hidden_sum = scatter_tokens(
        jnp.concatenate(
            [
                contract("lf,df->ld", grad_gate_up, w_hidden).astype(B16),
                pad_rank(
                    (ADAPTER_SCALING * contract("lf,rf->lr", grad_gate_up, diag_hidden)).astype(B16)
                ),
            ],
            axis=1,
        ),
        place,
    )
    grad_lowrank_hidden = hidden_sum[:, 2048 : 2048 + 2 * RANK].astype(B16)
    grad_left_hidden = contract("td,tr->dr", normed_two_b, grad_lowrank_hidden)
    grad_normed_two = hidden_sum[:, :2048] + contract(
        "tr,dr->td", grad_lowrank_hidden, picked_wide[:, 48:80]
    )
    grad_residual = upstream_b.astype(F32) + norm_backward(
        residual_one, scale_two, gain_values[1], grad_normed_two
    )

    grad_branch_b = grad_residual.astype(B16)
    grad_right_out = ADAPTER_SCALING * contract("td,tr->dr", grad_branch_b, lowrank_out_b)
    seq_grad_branch = gather_tokens(grad_branch_b, place)
    grad_lowrank_out = (ADAPTER_SCALING * product(seq_grad_branch, picked_wide)).astype(B16)[
        :, 80:96
    ]
    grad_attention_in = product(seq_grad_branch, w_out) + product(grad_lowrank_out, pick_out)
    grad_left_out = contract("lr,lc->rc", grad_lowrank_out, attention_b)
    grad_heads = grad_attention_in.reshape(length, heads_local, 2 * HEAD_DIM).transpose(1, 0, 2)
    grad_raw_b = norm_backward(raw_heads, head_factor, OUT_GAIN, grad_heads).astype(B16)

    def backward_head(head_items):
        query_pair, key_pair, values, lambda_one, log_total, grad_out = head_items
        return head_backward(
            query_pair, key_pair, values, lambda_one, log_total, grad_out, mask_bias
        )

    grad_query, grad_key, grad_value = lax.map(
        backward_head, (query_heads, key_heads, value_heads, lambda_all, log_totals, grad_raw_b)
    )
    grad_projected_b = jnp.concatenate(
        [
            grad_query.transpose(2, 0, 1, 3).reshape(length, -1),
            grad_key.transpose(2, 0, 1, 3).reshape(length, -1),
            grad_value.transpose(1, 0, 2).reshape(length, -1),
        ],
        axis=1,
    ).astype(B16)
    right_inputs = [
        ADAPTER_SCALING
        * contract(
            "lr,lc->rc",
            lowrank_inputs[:, RANK * i : RANK * (i + 1)],
            grad_projected_b[:, proj * i : proj * (i + 1)],
        )
        for i in range(3)
    ]
    input_sum = scatter_tokens(
        jnp.concatenate(
            [
                contract("lc,dc->ld", grad_projected_b, w_in).astype(B16),
                pad_rank(
                    (ADAPTER_SCALING * contract("lc,rc->lr", grad_projected_b, diag_in)).astype(B16)
                ),
            ],
            axis=1,
        ),
        place,
    )
    grad_lowrank_inputs = input_sum[:, 2048 : 2048 + 3 * RANK].astype(B16)
    grad_left_inputs = contract("td,tr->dr", normed_one_b, grad_lowrank_inputs)
    grad_normed_one = input_sum[:, :2048] + contract(
        "tr,dr->td", grad_lowrank_inputs, picked_wide[:, 0:48]
    )
    grad_input = grad_residual + norm_backward(
        local_tokens, scale_one, gain_values[0], grad_normed_one
    )

    wide_grads = jnp.concatenate(
        [
            grad_left_inputs,
            grad_left_hidden,
            grad_right_out,
            grad_right_down,
            jnp.zeros((2048, RANK), F32),
        ],
        axis=1,
    ).astype(B16)
    split_grads = jnp.concatenate(
        right_inputs + [grad_left_out] + right_hidden + [grad_left_down], axis=1
    ).astype(B16)
    columns = split_grads.shape[1]
    piece = -(-columns // 1024) * 128
    split_blocks = (
        jnp.pad(split_grads, ((0, 0), (0, 8 * piece - columns)))
        .reshape(4, 4, 2, 4, piece)
        .transpose(1, 2, 0, 3, 4)
        .reshape(128, piece // 128, 128)
    )
    blocks = jnp.concatenate(
        [
            wide_grads.reshape(128, 16, 128),
            split_blocks,
            jnp.broadcast_to(adapter.astype(B16), (128, 8 - piece // 128, 128)),
        ],
        axis=1,
    )
    arrived = lax.all_to_all(blocks, AXES, split_axis=0, concat_axis=0, tiled=True)
    ids_all = arrived.reshape(32, 4, 24, 128)[:, 0, 23, 0].astype(jnp.int32)
    member = ids_all[None, :] == jnp.arange(ADAPTERS)[:, None]
    onehot = member.astype(B16)
    wide_sum = contract(
        "es,sn->en",
        onehot,
        arrived[:, :16].reshape(32, 4 * 16 * 128),
    ).reshape(8, 4, 16, 128).sum(1)
    split_sum = contract(
        "es,sn->en", onehot, arrived[:, 16:].reshape(32, 4 * 8 * 128)
    ).reshape(8, 4, 8, 128)[:, :, : piece // 128]
    squares = jnp.sum(wide_sum * wide_sum) + jnp.sum(split_sum * split_sum)
    grads_wide = (
        wide_sum[:, :, :112].reshape(8, 16, 7, 16).transpose(2, 0, 3, 1).reshape(7, 128, 16)
    )
    mine = place.dp % 4
    split_out = jnp.concatenate(
        [split_sum.reshape(32, 7, 128), jnp.zeros((32, 1, 128), F32)], axis=1
    ).reshape(8, 1, 4, 8, 128)
    quarter = jnp.arange(4)[None, :, None, None, None]
    spread = jnp.where(quarter == mine, split_out, 0.0).reshape(128, 8, 128)
    spread = jnp.where(jnp.arange(8)[None, :, None] == 7, squares, spread)
    placed = lax.all_to_all(spread, AXES, split_axis=0, concat_axis=0, tiled=True)
    total_squares = jnp.sum(placed[:, 7, 0])
    from_mine = lax.dynamic_index_in_dim(
        placed.reshape(8, 4, 4, 8, 128), mine, 1, keepdims=False
    )
    split_rows = from_mine[:, :, :7].reshape(4, 8 * piece)[:, :columns]
    grads_attention = split_rows[:, : 4 * proj].reshape(4, 4, proj).transpose(1, 0, 2)
    grads_feedforward = split_rows[:, 4 * proj :].reshape(4, 3, ff).transpose(1, 0, 2)

    grad_norm = jnp.sqrt(total_squares)
    factor = CLIP_NORM / (grad_norm + 1e-06)
    wide_new = adam_step(adapter_wide, grads_wide, moment_wide, variance_wide, factor)
    attention_new = adam_step(
        adapter_attention, grads_attention, moment_attention, variance_attention, factor
    )
    feedforward_new = adam_step(
        adapter_feedforward, grads_feedforward, moment_feedforward, variance_feedforward, factor
    )
    return (
        result.astype(B16)[None],
        grad_input.astype(B16)[None],
        grad_norm,
        wide_new[0],
        attention_new[0],
        feedforward_new[0],
        wide_new[1],
        attention_new[1],
        feedforward_new[1],
        wide_new[2],
        attention_new[2],
        feedforward_new[2],
        wide_new[3],
        attention_new[3],
        feedforward_new[3],
    )


def solution(mesh):
    return jax.shard_map(
        local,
        mesh=mesh,
        in_specs=(
            P("dp", "tensor", None),
            P("dp", "tensor", None),
            P("dp"),
            P(),
            P(None, "tensor", None),
            P(None, "dp", "tensor"),
            P("tensor", "dp"),
            P(None, "dp", "tensor"),
            P("tensor", "dp"),
            P(None, None, ("dp", "tensor")),
            P(None, "dp", "tensor"),
            P(None, "dp", "tensor"),
            P(None, None, ("dp", "tensor")),
            P(None, None, ("dp", "tensor")),
            P(None, "dp", "tensor"),
            P(None, "dp", "tensor"),
            P(None, "dp", "tensor"),
            P(None, "dp", "tensor"),
        ),
        out_specs=(
            P("dp", "tensor", None),
            P("dp", "tensor", None),
            P(),
            P(None, None, ("dp", "tensor")),
            P(None, "dp", "tensor"),
            P(None, "dp", "tensor"),
            P(None, None, ("dp", "tensor")),
            P(None, "dp", "tensor"),
            P(None, "dp", "tensor"),
            P(None, None, ("dp", "tensor")),
            P(None, "dp", "tensor"),
            P(None, "dp", "tensor"),
            P(None, None, ("dp", "tensor")),
            P(None, "dp", "tensor"),
            P(None, "dp", "tensor"),
        ),
        check_vma=False,
    )
```

time: 2700 us -> 845 us (0.31)
  waiting for transfers between devices: 2180 us -> 300 us
  blocking collectives: 222 us -> 0 us
  starting transfers between devices: 1.39 us -> 125 us
  local copies, waits for them, and re-layouts: 62.4 us -> 176 us
    all_gather x10 -> x0, waiting for transfers between devices: 1010 us -> none  [the longest x1 233 us: local(): lax.all_gather(frozen_parts[2], 'dp', axis=1, tiled=True)]
    reduce_scatter x5 -> x0, waiting for transfers between devices: 822 us -> none  [the longest x1 642 us: local(): lax.psum_scatter(spread(wide_picked_grads, onehot), ('dp', 'tensor'), sca...]
    unnamed x25 -> x0, waiting for transfers between devices: 344 us -> none
    ppermute x0 -> x68, waiting for transfers between devices: none -> 280 us  [send(): return lax.ppermute(values, AXES, pairs)]
    all_gather x5 -> x0, blocking collectives: 153 us -> none  [the longest x1 73.8 us: local(): lax.all_gather(frozen_parts[4], 'dp', axis=1, tiled=True)]
    ppermute x0 -> x68, starting transfers between devices: none -> 112 us  [send(): return lax.ppermute(values, AXES, pairs)]
    dynamic_update_slice x0 -> x118, local copies, waits for them, and re-layouts: none -> 89.7 us  [put(): return lax.dynamic_update_slice(buffer, values, starts)]
    psum x1 -> x0, blocking collectives: 69.2 us -> none  [local(): total_squares = lax.psum(local_squares, ('dp', 'tensor'))]
  transfers between devices with their start and end apart: 20 -> 70, of which waited for: 18 -> 39; matrix products, arithmetic and copies ran while one was open for 8% -> 35% of each run, Pallas kernels for 0% -> 0%
where the time goes in v1:
time: 845 us; the launch traced here: 834 us
  waiting for transfers between devices  300 us (36%)
  local copies, waits for them, and re-layouts  176 us (21%)
  matrix products  168 us (20%)
  starting transfers between devices  125 us (15%)
  other arithmetic  55.8 us (7%)
    ppermute x68, waiting for transfers between devices, send(): return lax.ppermute(values, AXES, pairs)  280 us
    ppermute x68, starting transfers between devices, send(): return lax.ppermute(values, AXES, pairs)  112 us
    dot_general x36, matrix products, contract(): return jnp.einsum(form, left, right, preferred_element_type=F32)  107 us
    dynamic_update_slice x118, local copies, waits for them, and re-layouts, put(): return lax.dynamic_update_slice(buffer, values, starts)  89.7 us
    dot_general x15, matrix products, product(): return jnp.dot(left, right, preferred_element_type=F32)  60.6 us
    unnamed x243, local copies, waits for them, and re-layouts  19.5 us
  transfers between devices with their start and end apart: 70, of which 39 were waited for; matrix products, arithmetic and copies ran while one was open for 35% of the time, Pallas kernels for 0%

profile of v1, /device:TPU:1, one launch (start us, length us, event | category | flops | bytes accessed | tf_op | source)
XLA Modules:
  0.0 833.7 jit_solution(17119323190519700530)
XLA Ops:
  28.4 20.9 %collective-permute-done.41 = bf16[64,1536]{1,0:T(8,128)(2,1)S(1)} collective-permute-done((bf16[64,1536]{1,0:T(8,128)(2,1)S(1)}, bf16[64,1536]{1,0:T(8,128)(2,1)S(1)}, u32[]{:S(2)}, u32[]{:S(2)}) %collective-permute-start.41) | collective-permute-done | bytes 196640 | tf_op jit(solution)/shard_map/ppermute | solution.py:64
  115.8 8.2 collective-permute-done.6
  207.7 36.6 %collective-permute-start.2 = (bf16[192,2048]{1,0:T(8,128)(2,1)}, bf16[192,2048]{1,0:T(8,128)(2,1)S(1)}, u32[]{:S(2)}, u32[]{:S(2)}) collective-permute-start(bf16[192,2048]{1,0:T(8,128)(2,1)} %collective-permute-done.1), channel_id=1, source_target_pairs={{0,1},{1,0},{4,5},{5,4},{2,3},{3,2},{6,7},{7,6},{8,9},{9,8},{12,13... | collective-permute-start | bytes 2359304 | tf_op jit(solution)/shard_map/ppermute | solution.py:64
  246.4 11.2 %collective-permute-done.47 = bf16[2,2,32,1536]{3,2,1,0:T(8,128)(2,1)S(1)} collective-permute-done((bf16[2,2,32,1536]{3,2,1,0:T(8,128)(2,1)S(1)}, bf16[2,2,32,1536]{3,2,1,0:T(8,128)(2,1)S(1)}, u32[]{:S(2)}, u32[]{:S(2)}) %collective-permute-start.47) | collective-permute-done | bytes 393248 | tf_op jit(solution)/shard_map/ppermute | solution.py:64
  264.5 8.2 collective-permute-start.60
  277.3 11.0 %collective-permute-done.54 = bf16[2,2,32,1536]{3,2,1,0:T(8,128)(2,1)S(1)} collective-permute-done((bf16[2,2,32,1536]{3,2,1,0:T(8,128)(2,1)S(1)}, bf16[2,2,32,1536]{3,2,1,0:T(8,128)(2,1)S(1)}, u32[]{:S(2)}, u32[]{:S(2)}) %collective-permute-start.54) | collective-permute-done | bytes 393248 | tf_op jit(solution)/shard_map/ppermute | solution.py:64
  289.1 9.0 %collective-permute-done.55 = bf16[2,2,32,1536]{3,2,1,0:T(8,128)(2,1)S(1)} collective-permute-done((bf16[2,2,32,1536]{3,2,1,0:T(8,128)(2,1)S(1)}, bf16[2,2,32,1536]{3,2,1,0:T(8,128)(2,1)S(1)}, u32[]{:S(2)}, u32[]{:S(2)}) %collective-permute-start.55) | collective-permute-done | bytes 393248 | tf_op jit(solution)/shard_map/ppermute | solution.py:64
  312.0 13.3 %collective-permute-done.15 = bf16[4,2,32,2432]{3,2,1,0:T(8,128)(2,1)S(1)} collective-permute-done((bf16[4,2,32,2432]{3,2,1,0:T(8,128)(2,1)S(1)}, bf16[4,2,32,2432]{3,2,1,0:T(8,128)(2,1)S(1)}, u32[]{:S(2)}, u32[]{:S(2)}) %collective-permute-start.15) | collective-permute-done | bytes 1245216 | tf_op jit(solution)/shard_map/ppermute | solution.py:64
  325.4 10.5 %collective-permute-done.30 = bf16[4,2,32,3072]{3,2,1,0:T(8,128)(2,1)S(1)} collective-permute-done((bf16[4,2,32,3072]{3,2,1,0:T(8,128)(2,1)S(1)}, bf16[4,2,32,3072]{3,2,1,0:T(8,128)(2,1)S(1)}, u32[]{:S(2)}, u32[]{:S(2)}) %collective-permute-start.30) | collective-permute-done | bytes 1572896 | tf_op jit(solution)/shard_map/ppermute | solution.py:64
  343.9 15.1 %collective-permute-done.38 = bf16[4,2,32,3072]{3,2,1,0:T(8,128)(2,1)S(1)} collective-permute-done((bf16[4,2,32,3072]{3,2,1,0:T(8,128)(2,1)S(1)}, bf16[4,2,32,3072]{3,2,1,0:T(8,128)(2,1)S(1)}, u32[]{:S(2)}, u32[]{:S(2)}) %collective-permute-start.38) | collective-permute-done | bytes 1572896 | tf_op jit(solution)/shard_map/ppermute | solution.py:64
  444.7 11.3 %while.28 = (s32[]{:T(128)}, f32[2,768,256]{2,1,0:T(8,128)}, f32[2,2,768]{2,1,0:T(2,128)S(1)}, bf16[2,2,768,128]{3,2,1,0:T(8,128)(2,1)S(1)}, bf16[2,2,768,128]{3...) while((s32[]{:T(128)}, f32[2,768,256]{2,1,0:T(8,128)}, ...), condition=%wide.region_6.7_spmd.clone, body=%wide.region_3.6_spmd.clone.sunk | while | flops 619903488 | bytes 38196872 | solution.py:335
  480.6 16.5 %collective-permute-done.22 = bf16[192,2176]{1,0:T(8,128)(2,1)S(1)} collective-permute-done((bf16[192,2176]{1,0:T(8,128)(2,1)S(1)}, bf16[192,2176]{1,0:T(8,128)(2,1)S(1)}, u32[]{:S(2)}, u32[]{:S(2)}) %collective-permute-start.22) | collective-permute-done | bytes 835616 | tf_op jit(solution)/shard_map/ppermute | solution.py:64
  513.6 11.3 %collective-permute-done.24 = bf16[192,2048]{1,0:T(8,128)(2,1)} collective-permute-done((bf16[192,2048]{1,0:T(8,128)(2,1)}, bf16[192,2048]{1,0:T(8,128)(2,1)}, u32[]{:S(2)}, u32[]{:S(2)}) %collective-permute-start.24) | collective-permute-done | bytes 786464 | tf_op jit(solution)/shard_map/ppermute | solution.py:64
  535.3 16.3 %convolution_add_fusion = f32[768,2816]{1,0:T(8,128)} fusion(f32[768,2816]{1,0:T(8,128)S(1)} %fusion.228, bf16[768,2048]{1,0:T(8,128)(2,1)} %bitcast.133, bf16[2048,2816]{1,0:T(8,128)(2,1)} %bitcast.167), kind=kOutput, calls=%fused_computation.84 | convolution fusion | flops 8860532736 | bytes 31981568 | tf_op jit(solution)/shard_map/dot_general | solution.py:30
  551.6 11.8 %multiply_convert_fusion.1 = (bf16[768,1408]{1,0:T(8,128)(2,1)S(1)}, bf16[768,1408]{1,0:T(8,128)(2,1)S(1)}, bf16[768,1408]{1,0:T(8,128)(2,1)}) fusion(f32[768,2816]{1,0:T(8,128)} %convolution_add_fusion, f32[768,1408]{1,0:T(8,128)} %fusion.232, bf16[768,2048]{1,0:T(8,128)(2,1)} %bitcast.252, bf16[2048,1408]{1,0:T(8,128)(2,1)S(1)} %bitcast.971), kind=kOutput, calls=%fused_computation.88 | convolution fusion | flops 4447567872 | bytes 28377088 | tf_op jit(solution)/shard_map/dot_general | solution.py:30
  563.3 14.8 %convolution_convert_fusion.2 = bf16[768,2048]{1,0:T(8,128)(2,1)} fusion(bf16[2048,2816]{1,0:T(8,128)(2,1)} %bitcast.167, bf16[768,1408]{1,0:T(8,128)(2,1)S(1)} %get-tuple-element.266, bf16[768,1408]{1,0:T(8,128)(2,1)S(1)} %get-tuple-element.265), kind=kOutput, calls=%fused_computation.94 | convolution fusion | flops 8868593664 | bytes 19005440 | tf_op jit(solution)/shard_map/lf,df->ld/dot_general | solution.py:34
  585.1 9.3 %convolution_convert_fusion.3 = bf16[768,2048]{1,0:T(8,128)(2,1)} fusion(bf16[768,1408]{1,0:T(8,128)(2,1)S(1)} %copy-done.24, bf16[2048,1408]{1,0:T(8,128)(2,1)} %bitcast.968), kind=kOutput, calls=%fused_computation.95 | convolution fusion | flops 4430757888 | bytes 11075584 | tf_op jit(solution)/shard_map/lf,df->ld/dot_general | solution.py:34
  610.8 18.1 %collective-permute-done.62 = bf16[192,2176]{1,0:T(8,128)(2,1)S(1)} collective-permute-done((bf16[192,2176]{1,0:T(8,128)(2,1)S(1)}, bf16[192,2176]{1,0:T(8,128)(2,1)S(1)}, u32[]{:S(2)}, u32[]{:S(2)}) %collective-permute-start.62) | collective-permute-done | bytes 835616 | tf_op jit(solution)/shard_map/ppermute | solution.py:64
  643.9 12.1 %collective-permute-done.64 = bf16[192,2048]{1,0:T(8,128)(2,1)S(1)} collective-permute-done((bf16[192,2048]{1,0:T(8,128)(2,1)}, bf16[192,2048]{1,0:T(8,128)(2,1)S(1)}, u32[]{:S(2)}, u32[]{:S(2)}) %collective-permute-start.64) | collective-permute-done | bytes 786464 | tf_op jit(solution)/shard_map/ppermute | solution.py:64
  667.0 47.0 %while.29 = (s32[]{:T(128)}, bf16[2,2,768,128]{2,3,1,0:T(8,128)(2,1)}, bf16[2,2,768,128]{2,3,1,0:T(8,128)(2,1)}, bf16[2,768,256]{1,2,0:T(8,128)(2,1)}, bf16[2,2,...) while((s32[]{:T(128)}, ...), condition=%wide.region_13.14_spmd.clone, body=%wide.region_11.13_spmd.clone.sunk | while | flops 1532957184 | bytes 56259292 | solution.py:439
  714.1 9.9 %convolution_convert_fusion.1 = bf16[768,2048]{1,0:T(8,128)(2,1)} fusion(bf16[2048,1536]{1,0:T(8,128)(2,1)} %bitcast.43, bf16[768,512]{0,1:T(8,128)(2,1)} %bitcast.992, bf16[768,512]{0,1:T(8,128)(2,1)} %bitcast.989, bf16[768,512]{0,1:T(8,128)(2,1)} %bitcast.986), kind=kOutput, calls=%fused_computation.93 | convolution fusion | flops 4840488960 | bytes 11796480 | tf_op jit(solution)/shard_map/lc,dc->ld/dot_general | solution.py:34
  746.9 15.9 %collective-permute-done.67 = bf16[192,2176]{1,0:T(8,128)(2,1)} collective-permute-done((bf16[192,2176]{1,0:T(8,128)(2,1)S(1)}, bf16[192,2176]{1,0:T(8,128)(2,1)}, u32[]{:S(2)}, u32[]{:S(2)}) %collective-permute-start.67) | collective-permute-done | bytes 835616 | tf_op jit(solution)/shard_map/ppermute | solution.py:64
  784.7 10.0 %all-to-all-done = bf16[128,24,128]{2,1,0:T(8,128)(2,1)} async-done(((bf16[128,24,128]{2,1,0:T(8,128)(2,1)}), bf16[128,24,128]{2,1,0:T(8,128)(2,1)}, u32[]{:S(2)}, u32[]{:S(2)}) %all-to-all-start) | async-done | bytes 786464 | tf_op jit(solution)/shard_map/all_to_all | solution.py:509
  815.6 10.0 %all-to-all-done.1 = f32[128,8,128]{2,1,0:T(8,128)} async-done(((f32[128,8,128]{2,1,0:T(8,128)}), f32[128,8,128]{2,1,0:T(8,128)}, u32[]{:S(2)}, u32[]{:S(2)}) %all-to-all-start.1) | async-done | bytes 524320 | tf_op jit(solution)/shard_map/all_to_all | solution.py:532
  (733 shorter events, 525.0 us)
Async XLA Ops:
  5.7 185.1 %collective-permute-start = (bf16[192,2048]{1,0:T(8,128)(2,1)}, bf16[192,2048]{1,0:T(8,128)(2,1)}, u32[]{:S(2)}, u32[]{:S(2)}) collective-permute-start(bf16[192,2048]{1,0:T(8,128)(2,1)} %fusion.96), channel_id=1, source_target_pairs={{0,1},{1,0},{4,5},{5,4},{2,3},{3,2},{6,7},{7,6},{8,9},{9,8},{12,13... | collective-permute-start | bytes 2359304 | tf_op jit(solution)/shard_map/ppermute | solution.py:64
  7.2 190.2 %collective-permute-start.1 = (bf16[192,2048]{1,0:T(8,128)(2,1)}, bf16[192,2048]{1,0:T(8,128)(2,1)}, u32[]{:S(2)}, u32[]{:S(2)}) collective-permute-start(bf16[192,2048]{1,0:T(8,128)(2,1)} %fusion.96), channel_id=1, source_target_pairs={{0,2},{1,3},{4,6},{5,7},{2,0},{3,1},{6,4},{7,5},{8,10},{9,11},{12,... | collective-permute-start | bytes 2359304 | tf_op jit(solution)/shard_map/ppermute | solution.py:64
  10.0 185.2 %collective-permute-start.58 = (bf16[192,2048]{1,0:T(8,128)(2,1)}, bf16[192,2048]{1,0:T(8,128)(2,1)}, u32[]{:S(2)}, u32[]{:S(2)}) collective-permute-start(bf16[192,2048]{1,0:T(8,128)(2,1)} %bitcast.962), channel_id=1, source_target_pairs={{0,1},{1,0},{4,5},{5,4},{2,3},{3,2},{6,7},{7,6},{8,9},{9,8},{12,13... | collective-permute-start | bytes 2359304 | tf_op jit(solution)/shard_map/ppermute | solution.py:64
  10.3 191.8 %collective-permute-start.59 = (bf16[192,2048]{1,0:T(8,128)(2,1)}, bf16[192,2048]{1,0:T(8,128)(2,1)}, u32[]{:S(2)}, u32[]{:S(2)}) collective-permute-start(bf16[192,2048]{1,0:T(8,128)(2,1)} %bitcast.963), channel_id=1, source_target_pairs={{0,2},{1,3},{4,6},{5,7},{2,0},{3,1},{6,4},{7,5},{8,10},{9,11},{12,... | collective-permute-start | bytes 2359304 | tf_op jit(solution)/shard_map/ppermute | solution.py:64
  12.3 37.0 %collective-permute-start.41 = (bf16[64,1536]{1,0:T(8,128)(2,1)S(1)}, bf16[64,1536]{1,0:T(8,128)(2,1)S(1)}, u32[]{:S(2)}, u32[]{:S(2)}) collective-permute-start(bf16[64,1536]{1,0:T(8,128)(2,1)S(1)} %get-tuple-element.282), channel_id=1, source_target_pairs={{0,4},{1,5},{4,0},{5,1},{2,6},{3,7},{6,2},{7,3},{8,12},{9,13},{12,... | collective-permute-start | bytes 589832 | tf_op jit(solution)/shard_map/ppermute | solution.py:64
  197.3 47.9 %collective-permute-start.53 = (bf16[4,2,32,1536]{3,2,1,0:T(8,128)(2,1)S(1)}, bf16[4,2,32,1536]{3,2,1,0:T(8,128)(2,1)S(1)}, u32[]{:S(2)}, u32[]{:S(2)}) collective-permute-start(bf16[4,2,32,1536]{3,2,1,0:T(8,128)(2,1)S(1)} %bitcast_dynamic-update-slice_fusion.31), channel_id=1, source_target_pairs={{0,24},{1,25},{4,28},{5,29},{2,26},{3,27},{6,30},{7,31},{8,0},{9,1... | collective-permute-start | bytes 2359304 | tf_op jit(solution)/shard_map/ppermute | solution.py:64
  202.1 99.4 %collective-permute-start.7 = (bf16[4,2,32,2432]{3,2,1,0:T(8,128)(2,1)S(1)}, bf16[4,2,32,2432]{3,2,1,0:T(8,128)(2,1)S(1)}, u32[]{:S(2)}, u32[]{:S(2)}) collective-permute-start(bf16[4,2,32,2432]{3,2,1,0:T(8,128)(2,1)S(1)} %bitcast_dynamic-update-slice_fusion.27), channel_id=1, source_target_pairs={{0,32},{1,33},{4,36},{5,37},{2,34},{3,35},{6,38},{7,39},{8,40},{9,... | collective-permute-start | bytes 3735560 | tf_op jit(solution)/shard_map/ppermute | solution.py:64
  206.6 100.0 %collective-permute-start.8 = (bf16[4,2,32,2432]{3,2,1,0:T(8,128)(2,1)S(1)}, bf16[4,2,32,2432]{3,2,1,0:T(8,128)(2,1)S(1)}, u32[]{:S(2)}, u32[]{:S(2)}) collective-permute-start(bf16[4,2,32,2432]{3,2,1,0:T(8,128)(2,1)S(1)} %bitcast_dynamic-update-slice_fusion.27), channel_id=1, source_target_pairs={{0,96},{1,97},{4,100},{5,101},{2,98},{3,99},{6,102},{7,103},{8,104... | collective-permute-start | bytes 3735560 | tf_op jit(solution)/shard_map/ppermute | solution.py:64
  207.5 101.6 %collective-permute-start.14 = (bf16[4,2,32,2432]{3,2,1,0:T(8,128)(2,1)S(1)}, bf16[4,2,32,2432]{3,2,1,0:T(8,128)(2,1)S(1)}, u32[]{:S(2)}, u32[]{:S(2)}) collective-permute-start(bf16[4,2,32,2432]{3,2,1,0:T(8,128)(2,1)S(1)} %bitcast_dynamic-update-slice_fusion.23), channel_id=1, source_target_pairs={{0,8},{1,9},{4,12},{5,13},{2,10},{3,11},{6,14},{7,15},{8,16},{9,17... | collective-permute-start | bytes 3735560 | tf_op jit(solution)/shard_map/ppermute | solution.py:64
  207.7 68.7 %collective-permute-start.2 = (bf16[192,2048]{1,0:T(8,128)(2,1)}, bf16[192,2048]{1,0:T(8,128)(2,1)S(1)}, u32[]{:S(2)}, u32[]{:S(2)}) collective-permute-start(bf16[192,2048]{1,0:T(8,128)(2,1)} %collective-permute-done.1), channel_id=1, source_target_pairs={{0,1},{1,0},{4,5},{5,4},{2,3},{3,2},{6,7},{7,6},{8,9},{9,8},{12,13... | collective-permute-start | bytes 2359304 | tf_op jit(solution)/shard_map/ppermute | solution.py:64
  264.5 35.9 %collective-permute-start.60 = (bf16[192,2048]{1,0:T(8,128)(2,1)}, bf16[192,2048]{1,0:T(8,128)(2,1)S(1)}, u32[]{:S(2)}, u32[]{:S(2)}) collective-permute-start(bf16[192,2048]{1,0:T(8,128)(2,1)} %collective-permute-done.59), channel_id=1, source_target_pairs={{0,1},{1,0},{4,5},{5,4},{2,3},{3,2},{6,7},{7,6},{8,9},{9,8},{12,13... | collective-permute-start | bytes 2359304 | tf_op jit(solution)/shard_map/ppermute | solution.py:64
  300.5 35.5 %collective-permute-start.30 = (bf16[4,2,32,3072]{3,2,1,0:T(8,128)(2,1)S(1)}, bf16[4,2,32,3072]{3,2,1,0:T(8,128)(2,1)S(1)}, u32[]{:S(2)}, u32[]{:S(2)}) collective-permute-start(bf16[4,2,32,3072]{3,2,1,0:T(8,128)(2,1)S(1)} %bitcast_dynamic-update-slice_fusion.19), channel_id=1, source_target_pairs={{0,32},{1,33},{4,36},{5,37},{2,34},{3,35},{6,38},{7,39},{8,40},{9,... | collective-permute-start | bytes 4718600 | tf_op jit(solution)/shard_map/ppermute | solution.py:64
  301.5 35.7 %collective-permute-start.31 = (bf16[4,2,32,3072]{3,2,1,0:T(8,128)(2,1)S(1)}, bf16[4,2,32,3072]{3,2,1,0:T(8,128)(2,1)S(1)}, u32[]{:S(2)}, u32[]{:S(2)}) collective-permute-start(bf16[4,2,32,3072]{3,2,1,0:T(8,128)(2,1)S(1)} %bitcast_dynamic-update-slice_fusion.19), channel_id=1, source_target_pairs={{0,96},{1,97},{4,100},{5,101},{2,98},{3,99},{6,102},{7,103},{8,104... | collective-permute-start | bytes 4718600 | tf_op jit(solution)/shard_map/ppermute | solution.py:64
  306.6 34.9 %collective-permute-start.37 = (bf16[4,2,32,3072]{3,2,1,0:T(8,128)(2,1)S(1)}, bf16[4,2,32,3072]{3,2,1,0:T(8,128)(2,1)S(1)}, u32[]{:S(2)}, u32[]{:S(2)}) collective-permute-start(bf16[4,2,32,3072]{3,2,1,0:T(8,128)(2,1)S(1)} %bitcast_dynamic-update-slice_fusion.15), channel_id=1, source_target_pairs={{0,8},{1,9},{4,12},{5,13},{2,10},{3,11},{6,14},{7,15},{8,16},{9,17... | collective-permute-start | bytes 4718600 | tf_op jit(solution)/shard_map/ppermute | solution.py:64
  309.1 49.9 %collective-permute-start.38 = (bf16[4,2,32,3072]{3,2,1,0:T(8,128)(2,1)S(1)}, bf16[4,2,32,3072]{3,2,1,0:T(8,128)(2,1)S(1)}, u32[]{:S(2)}, u32[]{:S(2)}) collective-permute-start(bf16[4,2,32,3072]{3,2,1,0:T(8,128)(2,1)S(1)} %bitcast_dynamic-update-slice_fusion.15), channel_id=1, source_target_pairs={{0,24},{1,25},{4,28},{5,29},{2,26},{3,27},{6,30},{7,31},{8,0},{9,1... | collective-permute-start | bytes 4718600 | tf_op jit(solution)/shard_map/ppermute | solution.py:64
  325.3 34.8 %collective-permute-start.9 = (bf16[2,2,32,2432]{3,2,1,0:T(8,128)(2,1)S(1)}, bf16[2,2,32,2432]{3,2,1,0:T(8,128)(2,1)S(1)}, u32[]{:S(2)}, u32[]{:S(2)}) collective-permute-start(bf16[2,2,32,2432]{3,2,1,0:T(8,128)(2,1)S(1)} %slice.658), channel_id=1, source_target_pairs={{0,32},{1,33},{4,36},{5,37},{2,34},{3,35},{6,38},{7,39},{8,40},{9,... | collective-permute-start | bytes 1867784 | tf_op jit(solution)/shard_map/ppermute | solution.py:64
  335.9 27.6 %collective-permute-start.10 = (bf16[2,2,32,2432]{3,2,1,0:T(8,128)(2,1)S(1)}, bf16[2,2,32,2432]{3,2,1,0:T(8,128)(2,1)S(1)}, u32[]{:S(2)}, u32[]{:S(2)}) collective-permute-start(bf16[2,2,32,2432]{3,2,1,0:T(8,128)(2,1)S(1)} %slice.660), channel_id=1, source_target_pairs={{0,96},{1,97},{4,100},{5,101},{2,98},{3,99},{6,102},{7,103},{8,104... | collective-permute-start | bytes 1867784 | tf_op jit(solution)/shard_map/ppermute | solution.py:64
  337.2 30.2 %collective-permute-start.16 = (bf16[2,2,32,2432]{3,2,1,0:T(8,128)(2,1)S(1)}, bf16[2,2,32,2432]{3,2,1,0:T(8,128)(2,1)S(1)}, u32[]{:S(2)}, u32[]{:S(2)}) collective-permute-start(bf16[2,2,32,2432]{3,2,1,0:T(8,128)(2,1)S(1)} %slice.666), channel_id=1, source_target_pairs={{0,8},{1,9},{4,12},{5,13},{2,10},{3,11},{6,14},{7,15},{8,16},{9,17... | collective-permute-start | bytes 1867784 | tf_op jit(solution)/shard_map/ppermute | solution.py:64
  341.5 30.9 %collective-permute-start.17 = (bf16[2,2,32,2432]{3,2,1,0:T(8,128)(2,1)S(1)}, bf16[2,2,32,2432]{3,2,1,0:T(8,128)(2,1)S(1)}, u32[]{:S(2)}, u32[]{:S(2)}) collective-permute-start(bf16[2,2,32,2432]{3,2,1,0:T(8,128)(2,1)S(1)} %slice.668), channel_id=1, source_target_pairs={{0,24},{1,25},{4,28},{5,29},{2,26},{3,27},{6,30},{7,31},{8,0},{9,1... | collective-permute-start | bytes 1867784 | tf_op jit(solution)/shard_map/ppermute | solution.py:64
  359.0 34.1 %collective-permute-start.32 = (bf16[2,2,32,3072]{3,2,1,0:T(8,128)(2,1)}, bf16[2,2,32,3072]{3,2,1,0:T(8,128)(2,1)}, u32[]{:S(2)}, u32[]{:S(2)}) collective-permute-start(bf16[2,2,32,3072]{3,2,1,0:T(8,128)(2,1)} %slice.715), channel_id=1, source_target_pairs={{0,32},{1,33},{4,36},{5,37},{2,34},{3,35},{6,38},{7,39},{8,40},{9,... | collective-permute-start | bytes 2359304 | tf_op jit(solution)/shard_map/ppermute | solution.py:64
  360.1 34.5 %collective-permute-start.33 = (bf16[2,2,32,3072]{3,2,1,0:T(8,128)(2,1)}, bf16[2,2,32,3072]{3,2,1,0:T(8,128)(2,1)}, u32[]{:S(2)}, u32[]{:S(2)}) collective-permute-start(bf16[2,2,32,3072]{3,2,1,0:T(8,128)(2,1)} %slice.717), channel_id=1, source_target_pairs={{0,96},{1,97},{4,100},{5,101},{2,98},{3,99},{6,102},{7,103},{8,104... | collective-permute-start | bytes 2359304 | tf_op jit(solution)/shard_map/ppermute | solution.py:64
  363.5 109.7 %collective-permute-start.39 = (bf16[2,2,32,3072]{3,2,1,0:T(8,128)(2,1)}, bf16[2,2,32,3072]{3,2,1,0:T(8,128)(2,1)}, u32[]{:S(2)}, u32[]{:S(2)}) collective-permute-start(bf16[2,2,32,3072]{3,2,1,0:T(8,128)(2,1)} %slice.723), channel_id=1, source_target_pairs={{0,8},{1,9},{4,12},{5,13},{2,10},{3,11},{6,14},{7,15},{8,16},{9,17... | collective-permute-start | bytes 2359304 | tf_op jit(solution)/shard_map/ppermute | solution.py:64
  367.4 111.2 %collective-permute-start.40 = (bf16[2,2,32,3072]{3,2,1,0:T(8,128)(2,1)}, bf16[2,2,32,3072]{3,2,1,0:T(8,128)(2,1)}, u32[]{:S(2)}, u32[]{:S(2)}) collective-permute-start(bf16[2,2,32,3072]{3,2,1,0:T(8,128)(2,1)} %slice.725), channel_id=1, source_target_pairs={{0,24},{1,25},{4,28},{5,29},{2,26},{3,27},{6,30},{7,31},{8,0},{9,1... | collective-permute-start | bytes 2359304 | tf_op jit(solution)/shard_map/ppermute | solution.py:64
  637.4 91.3 %collective-permute-start.57 = (bf16[192,2176]{1,0:T(8,128)(2,1)}, bf16[192,2176]{1,0:T(8,128)(2,1)}, u32[]{:S(2)}, u32[]{:S(2)}) collective-permute-start(bf16[192,2176]{1,0:T(8,128)(2,1)} %fusion.130), channel_id=1, source_target_pairs={{0,2},{1,3},{4,6},{5,7},{2,0},{3,1},{6,4},{7,5},{8,10},{9,11},{12,... | collective-permute-start | bytes 2506760 | tf_op jit(solution)/shard_map/ppermute | solution.py:64
  (166 other events, 2300.0 us)

commit v2 on v1

v2 whole, which is shorter than its diff:
```python
import jax
import jax.numpy as jnp
from jax import lax
from jax.experimental import pallas as pl
from jax.experimental.pallas import tpu as pltpu
from jax.sharding import PartitionSpec as P

HEAD_DIM = 128
ADAPTERS = 8
RANK = 16
BLOCK = 256
STEP = 10


NORM_EPS = 1e-05
ADAPTER_SCALING = 0.5
LAMBDA_INIT = 0.2
OUT_GAIN = 0.8
CLIP_NORM = 1.0
LEARN_RATE = 0.05
BETA_FIRST = 0.9
BETA_SECOND = 0.999
ADAM_EPS = 1e-08
WEIGHT_DECAY = 0.01
NEG_LARGE = -1e30
AXES = ("dp", "tensor")
B16 = jnp.bfloat16
F32 = jnp.float32


def product(left, right):
    return jnp.dot(left, right, preferred_element_type=F32)


def contract(form, left, right):
    return jnp.einsum(form, left, right, preferred_element_type=F32)


def index_of(z, y, x, core):
    x, y, z, core = x % 4, y % 4, z % 4, core % 2
    return ((z * 4 + y) * 2 + x % 2) * 4 + (x // 2) * 2 + core


def routes(move):
    pairs = []
    for z in range(4):
        for y in range(4):
            for x in range(4):
                for core in range(2):
                    pairs.append((index_of(z, y, x, core), index_of(*move(z, y, x, core))))
    return pairs


UP_Z = routes(lambda z, y, x, c: (z + 1, y, x, c))
DOWN_Z = routes(lambda z, y, x, c: (z - 1, y, x, c))
FAR_Z = routes(lambda z, y, x, c: (z + 2, y, x, c))
UP_Y = routes(lambda z, y, x, c: (z, y + 1, x, c))
DOWN_Y = routes(lambda z, y, x, c: (z, y - 1, x, c))
FAR_Y = routes(lambda z, y, x, c: (z, y + 2, x, c))
PAIR_X = routes(lambda z, y, x, c: (z, y, x ^ 1, c))
FAR_X = routes(lambda z, y, x, c: (z, y, x + 2, c))
CORES = routes(lambda z, y, x, c: (z, y, x, 1 - c))


def send(values, pairs):
    return lax.ppermute(values, AXES, pairs)


class Place:
    def __init__(self):
        tensor = lax.axis_index("tensor")
        self.far, self.core, self.tensor = tensor // 2, tensor % 2, tensor
        self.dp = lax.axis_index("dp")


def together(*values):
    return lax.optimization_barrier(values)


OFFSETS = (0, 3, 1, 2)


def assemble(pieces_a, pieces_b, widths):
    half = pieces_a[0].shape[1]
    rows = 64 * half

    def kernel(*refs):
        sources, outs, sem = (refs[:5], refs[5:10]), refs[10:-1], refs[-1]
        dp = lax.axis_index("dp")
        at = (dp // 8, (dp // 2) & 3)
        x = dp & 1
        copies = []
        for order in range(2):
            for outer in range(4):
                for block in range(8):
                    places = [0, 0]
                    places[order] = (at[order] + OFFSETS[outer]) & 3
                    places[1 - order] = (at[1 - order] + OFFSETS[block // 2]) & 3
                    index = (places[0] * 4 + places[1]) * 2 + (x ^ (block % 2))
                    row = pl.multiple_of(index * (2 * half) + order * half, half)
                    if outer < 3:
                        source = sources[order][outer].at[block]
                    else:
                        source = sources[order][3 + block // 4].at[block % 4]
                    start = 0
                    for out, width in zip(outs, widths):
                        copy = pltpu.make_async_copy(
                            source.at[:, pl.ds(start, width)], out.at[pl.ds(row, half), :], sem
                        )
                        copy.start()
                        copies.append(copy)
                        start += width
        for copy in copies:
            copy.wait()

    return pl.pallas_call(
        kernel,
        out_shape=[jax.ShapeDtypeStruct((rows, width), B16) for width in widths],
        in_specs=[pl.BlockSpec(memory_space=pl.ANY)] * 10,
        out_specs=[pl.BlockSpec(memory_space=pl.ANY)] * len(widths),
        scratch_shapes=[pltpu.SemaphoreType.DMA],
        cost_estimate=pl.CostEstimate(
            flops=0, bytes_accessed=4 * rows * sum(widths), transcendentals=0
        ),
    )(*pieces_a, *pieces_b)


def first_blocks(shard, other):
    half = shard.shape[0] // 2
    return (jnp.stack([shard[:half], other[:half]]), jnp.stack([shard[half:], other[half:]]))


def ring_sends(part_a, part_b):
    return [(part_a, UP_Y), (part_a, DOWN_Y), (part_b, UP_Z), (part_b, DOWN_Z)]


def plane_sends(part_a, part_b):
    return [(part_a, UP_Z), (part_a, DOWN_Z), (part_b, UP_Y), (part_b, DOWN_Y)]


def relay_sends(sends, arrived):
    out = []
    for i, (_, pairs) in enumerate(sends):
        middle = arrived[i].shape[0] // 2
        out.append((arrived[i][:middle] if i % 2 == 0 else arrived[i][middle:], pairs))
    return out


def planes(part_a, part_b, near, far):
    return (
        jnp.concatenate([part_a, near[0], near[1], far[0], far[1]], axis=0),
        jnp.concatenate([part_b, near[2], near[3], far[2], far[3]], axis=0),
    )


def exchange(sends, *others):
    results = [send(values, pairs) for values, pairs in sends]
    out = together(*results, *others)
    return list(out[: len(sends)]), list(out[len(sends) :])


def in_place(values, place, axis=0):
    own, core, far, far_core = values
    swap_core, swap_far = place.core == 1, place.far == 1
    near = jnp.stack([jnp.where(swap_core, core, own), jnp.where(swap_core, own, core)])
    away = jnp.stack([jnp.where(swap_core, far_core, far), jnp.where(swap_core, far, far_core)])
    return jnp.concatenate(
        [jnp.where(swap_far, away, near), jnp.where(swap_far, near, away)], axis=0
    )


def scatter_tokens(near, away):
    sent = send(away().astype(B16), CORES)
    summed = near() + sent.astype(F32)
    rows = summed.shape[0] // 2
    return summed[:rows] + send(summed[rows:].astype(B16), FAR_X).astype(F32)


def norm_forward(values, gain_value):
    factor = lax.rsqrt(jnp.mean(values * values, axis=-1, keepdims=True) + NORM_EPS)
    return (values * factor * gain_value, factor)


def norm_backward(values, factor, gain_value, gradient):
    scaled = gradient * gain_value
    return factor * (
        scaled - values * factor * factor * jnp.mean(scaled * values, axis=-1, keepdims=True)
    )


TRANSPOSED_RIGHT = (((1,), (1,)), ((), ()))
TRANSPOSED_LEFT = (((0,), (0,)), ((), ()))


def dot_of(left, right, dims):
    return lax.dot_general(left, right, dims, preferred_element_type=F32)


def quarter_places(own, rows):
    return [pl.multiple_of((own ^ t) * rows, rows) for t in range(4)]


def attention_forward(own, lambda_all, near, far, heads):
    half, width = near.shape
    length, proj = 2 * half, width // 3
    rows = half // 2

    def kernel(own_ref, lambda_ref, near_ref, far_ref, att_ref, raw_ref, lse_ref, qkv_ref):
        for t in range(4):
            at = own_ref[0] ^ t
            start = pl.multiple_of((at & 1) * rows, rows)

            @pl.when(at < 2)
            def _():
                qkv_ref[t * rows : (t + 1) * rows, :] = near_ref[pl.ds(start, rows), :]

            @pl.when(at >= 2)
            def _():
                qkv_ref[t * rows : (t + 1) * rows, :] = far_ref[pl.ds(start, rows), :]

        for head in range(heads):
            column = head * 2 * HEAD_DIM
            value_columns = slice(2 * proj + column, 2 * proj + column + 2 * HEAD_DIM)
            for block in range(length // BLOCK):
                queries = slice(block * BLOCK, (block + 1) * BLOCK)
                keys = slice(0, (block + 1) * BLOCK)
                parts = []
                for c in range(2):
                    first = column + c * HEAD_DIM
                    scores = (
                        dot_of(
                            qkv_ref[keys, proj + first : proj + first + HEAD_DIM],
                            qkv_ref[queries, first : first + HEAD_DIM],
                            TRANSPOSED_RIGHT,
                        )
                        * HEAD_DIM**-0.5
                    )
                    top = jnp.max(scores, axis=0, keepdims=True)
                    shifted = jnp.exp(scores - top)
                    total = jnp.sum(shifted, axis=0, keepdims=True)
                    lse_ref[head * 2 + c : head * 2 + c + 1, queries] = top + jnp.log(total)
                    parts.append(shifted * (1.0 / total))
                combined = (parts[0] - lambda_ref[head] * parts[1]).astype(B16)
                raw = dot_of(combined, qkv_ref[keys, value_columns], TRANSPOSED_LEFT)
                raw_ref[queries, column : column + 2 * HEAD_DIM] = raw
        for t in range(4):
            start = pl.multiple_of((own_ref[0] ^ t) * rows, rows)
            for head in range(heads):
                columns = slice(head * 2 * HEAD_DIM, (head + 1) * 2 * HEAD_DIM)
                raw = raw_ref[t * rows : (t + 1) * rows, columns]
                factor = lax.rsqrt(jnp.mean(raw * raw, axis=-1, keepdims=True) + NORM_EPS)
                att_ref[pl.ds(start, rows), columns] = (raw * factor * OUT_GAIN).astype(B16)

    vmem = pl.BlockSpec(memory_space=pltpu.VMEM)
    smem = pl.BlockSpec(memory_space=pltpu.SMEM)
    return pl.pallas_call(
        kernel,
        out_shape=[
            jax.ShapeDtypeStruct((length, proj), B16),
            jax.ShapeDtypeStruct((length, proj), F32),
            jax.ShapeDtypeStruct((2 * heads, length), F32),
            jax.ShapeDtypeStruct((length, width), B16),
        ],
        in_specs=[smem, smem, vmem, vmem],
        out_specs=[vmem] * 4,
        compiler_params=pltpu.CompilerParams(vmem_limit_bytes=40 * 2**20),
        cost_estimate=pl.CostEstimate(
            flops=4 * length * length * proj, bytes_accessed=12 * length * width, transcendentals=2 * length * length * heads
        ),
    )(own, lambda_all, near, far)


def attention_backward(own, lambda_all, qkv, raw, lse, grad_near, grad_far, heads):
    length, width = qkv.shape
    proj, rows = width // 3, length // 4

    def kernel(
        own_ref, lambda_ref, qkv_ref, raw_ref, lse_ref, near_ref, far_ref, out_ref, graw_ref, acc_ref
    ):
        for t in range(4):
            at = own_ref[0] ^ t
            start = pl.multiple_of((at & 1) * rows, rows)

            def branch(source):
                for head in range(heads):
                    columns = slice(head * 2 * HEAD_DIM, (head + 1) * 2 * HEAD_DIM)
                    values = raw_ref[t * rows : (t + 1) * rows, columns]
                    factor = lax.rsqrt(
                        jnp.mean(values * values, axis=-1, keepdims=True) + NORM_EPS
                    )
                    grad = norm_backward(
                        values, factor, OUT_GAIN, source[pl.ds(start, rows), columns]
                    )
                    graw_ref[t * rows : (t + 1) * rows, columns] = grad.astype(B16)

            @pl.when(at < 2)
            def _():
                branch(near_ref)

            @pl.when(at >= 2)
            def _():
                branch(far_ref)

        for head in range(heads):
            column = head * 2 * HEAD_DIM
            value_columns = slice(2 * proj + column, 2 * proj + column + 2 * HEAD_DIM)
            key_columns = slice(proj + column, proj + column + 2 * HEAD_DIM)
            for block in reversed(range(length // BLOCK)):
                queries = slice(block * BLOCK, (block + 1) * BLOCK)
                keys = slice(0, (block + 1) * BLOCK)
                graw = graw_ref[queries, column : column + 2 * HEAD_DIM]
                probs = []
                for c in range(2):
                    first = column + c * HEAD_DIM
                    scores = (
                        dot_of(
                            qkv_ref[keys, proj + first : proj + first + HEAD_DIM],
                            qkv_ref[queries, first : first + HEAD_DIM],
                            TRANSPOSED_RIGHT,
                        )
                        * HEAD_DIM**-0.5
                    )
                    probs.append(
                        jnp.exp(scores - lse_ref[head * 2 + c : head * 2 + c + 1, queries])
                    )
                lambda_one = lambda_ref[head]
                combined = (probs[0] - lambda_one * probs[1]).astype(B16)
                grad_values = product(combined, graw)
                grad_combined = dot_of(qkv_ref[keys, value_columns], graw, TRANSPOSED_RIGHT)
                grad_keys = []
                for c in range(2):
                    first = column + c * HEAD_DIM
                    weighted = probs[c] * grad_combined
                    inner = jnp.sum(weighted, axis=0, keepdims=True)
                    scale = HEAD_DIM**-0.5 if c == 0 else -lambda_one * HEAD_DIM**-0.5
                    grad_scores = ((weighted - probs[c] * inner) * scale).astype(B16)
                    grad_keys.append(product(grad_scores, qkv_ref[queries, first : first + HEAD_DIM]))
                    acc_ref[queries, first : first + HEAD_DIM] = dot_of(
                        grad_scores,
                        qkv_ref[keys, proj + first : proj + first + HEAD_DIM],
                        TRANSPOSED_LEFT,
                    )
                grad_key = jnp.concatenate(grad_keys, axis=1)
                if block == length // BLOCK - 1:
                    acc_ref[keys, key_columns] = grad_key
                    acc_ref[keys, value_columns] = grad_values
                else:
                    acc_ref[keys, key_columns] += grad_key
                    acc_ref[keys, value_columns] += grad_values
        for t in range(4):
            start = pl.multiple_of((own_ref[0] ^ t) * rows, rows)
            out_ref[pl.ds(start, rows), :] = acc_ref[t * rows : (t + 1) * rows, :].astype(B16)

    vmem = pl.BlockSpec(memory_space=pltpu.VMEM)
    smem = pl.BlockSpec(memory_space=pltpu.SMEM)
    return pl.pallas_call(
        kernel,
        out_shape=jax.ShapeDtypeStruct((length, width), B16),
        in_specs=[smem, smem] + [vmem] * 5,
        out_specs=vmem,
        scratch_shapes=[pltpu.VMEM((length, proj), B16), pltpu.VMEM((length, width), F32)],
        compiler_params=pltpu.CompilerParams(vmem_limit_bytes=48 * 2**20),
        cost_estimate=pl.CostEstimate(
            flops=10 * length * length * proj, bytes_accessed=14 * length * width, transcendentals=2 * length * length * heads
        ),
    )(own, lambda_all, qkv, raw, lse, grad_near, grad_far)


def adam_step(parameter, gradient, moment, variance, factor):
    clipped = gradient * factor
    moment_new = BETA_FIRST * moment + (1.0 - BETA_FIRST) * clipped
    variance_new = BETA_SECOND * variance + (1.0 - BETA_SECOND) * clipped * clipped
    moment_hat = moment_new / (1.0 - BETA_FIRST**STEP)
    variance_hat = variance_new / (1.0 - BETA_SECOND**STEP)
    updated = parameter - LEARN_RATE * (
        moment_hat / (jnp.sqrt(variance_hat) + ADAM_EPS) + WEIGHT_DECAY * parameter
    )
    return (clipped, updated, moment_new, variance_new)


def flat_rows(stacked):
    moved = stacked.astype(B16).transpose(1, 0, 2)
    return moved.reshape(stacked.shape[1], -1)


def fold_rows(rows, lanes):
    padded = jnp.pad(rows, ((0, 0), (0, 16 * lanes - rows.shape[1])))
    return padded.reshape(64, lanes)


def pick_rows(gathered, adapter, width):
    lanes = gathered.shape[1]
    mine = lax.dynamic_slice_in_dim(gathered, adapter * 256, 256, 0)
    return mine.reshape(16, 16 * lanes)[:, :width]


def local(
    tokens,
    cotangent,
    adapter_ids,
    norm_gains,
    lambda_vectors,
    weight_inputs,
    weight_output,
    hidden_weight_matrix,
    weight_down,
    adapter_wide,
    adapter_attention,
    adapter_feedforward,
    moment_wide,
    variance_wide,
    moment_attention,
    variance_attention,
    moment_feedforward,
    variance_feedforward,
):
    place = Place()
    adapter = adapter_ids[0]
    own_quarter = place.tensor.astype(jnp.int32).reshape(1)
    local_tokens = tokens[0].astype(F32)
    upstream_b = cotangent[0]
    gain_values = norm_gains.astype(F32)
    lambda_all = (
        jnp.exp(jnp.sum(lambda_vectors[0] * lambda_vectors[1], axis=-1))
        - jnp.exp(jnp.sum(lambda_vectors[2] * lambda_vectors[3], axis=-1))
        + LAMBDA_INIT
    )
    heads_local = lambda_vectors.shape[1]
    proj = weight_inputs.shape[2]
    ff = hidden_weight_matrix.shape[2]
    rows = tokens.shape[1]

    wide_flat = jnp.pad(
        adapter_wide.astype(B16).transpose(0, 2, 1).reshape(112, 128), ((0, 16), (0, 0))
    )
    shard_one = jnp.concatenate(
        [
            weight_inputs[0],
            weight_inputs[1],
            weight_inputs[2],
            weight_output.T,
            fold_rows(flat_rows(adapter_attention), 128),
            wide_flat[:64],
            wide_flat[64:],
        ],
        axis=1,
    )
    shard_two = jnp.concatenate(
        [
            hidden_weight_matrix[0],
            hidden_weight_matrix[1],
            weight_down.T,
            fold_rows(flat_rows(adapter_feedforward), 384),
        ],
        axis=1,
    )
    normed_one, scale_one = norm_forward(local_tokens, gain_values[0])
    normed_one_b = normed_one.astype(B16)

    (other_one, core_normed), (shard_one, shard_two, upstream_b) = exchange(
        [(shard_one, PAIR_X), (normed_one_b, CORES)], shard_one, shard_two, upstream_b
    )
    blocks_one = first_blocks(shard_one, other_one)
    sends = ring_sends(*blocks_one)
    (*near, other_two), (upstream_b, normed_out) = exchange(
        sends + [(shard_two, PAIR_X)], upstream_b, normed_one_b
    )
    (*far, core_upstream), (normed_out, upstream_b) = exchange(
        relay_sends(sends, near) + [(upstream_b, CORES)], normed_out, upstream_b
    )
    planes_one = planes(*blocks_one, near, far)
    sends = plane_sends(*planes_one)
    (*near_one, far_normed), (upstream_b,) = exchange(sends + [(normed_out, FAR_X)], upstream_b)
    (*far_one, far_upstream), (shard_two, other_two) = exchange(
        relay_sends(sends, near_one) + [(upstream_b, FAR_X)], shard_two, other_two
    )
    w_in, w_out, fold_one = assemble(
        (planes_one[0], near_one[0], near_one[1], far_one[0], far_one[1]),
        (planes_one[1], near_one[2], near_one[3], far_one[2], far_one[3]),
        (3 * proj, proj, 384),
    )
    blocks_two = first_blocks(shard_two, other_two)
    sends = ring_sends(*blocks_two)
    near, _ = exchange(sends)
    far, _ = exchange(relay_sends(sends, near))
    planes_two = planes(*blocks_two, near, far)
    sends = plane_sends(*planes_two)
    near_two, _ = exchange(sends)
    far_two, _ = exchange(relay_sends(sends, near_two))
    w_hidden, w_down, fold_two = assemble(
        (planes_two[0], near_two[0], near_two[1], far_two[0], far_two[1]),
        (planes_two[1], near_two[2], near_two[3], far_two[2], far_two[3]),
        (2 * ff, ff, 384),
    )
    pick_attention = pick_rows(fold_one[:, :128], adapter, 4 * proj)
    pick_feedforward = pick_rows(fold_two, adapter, 3 * ff)
    pick_hidden, pick_down = pick_feedforward[:, : 2 * ff], pick_feedforward[:, 2 * ff :]

    onehot_rows = (
        jnp.arange(128)[None, :, None]
        == (adapter * RANK + jnp.arange(128) - RANK * jnp.arange(8)[:, None])[:, None, :]
    ) & (jnp.arange(128)[None, None, :] // RANK == jnp.arange(8)[:, None, None])
    wide_mine = (
        fold_one[:, 128:].reshape(32, 4, 16, 2, 128).transpose(0, 2, 3, 1, 4).reshape(512, 1024)
    )
    picked_t = product(wide_mine, onehot_rows.astype(B16).reshape(1024, 128)).astype(B16)
    picked_far = send(picked_t, FAR_X)
    picked_all = in_place(
        [picked_t, send(picked_t, CORES), picked_far, send(picked_far, CORES)], place
    ).reshape(4, 32, 16, 128)
    picked_wide = picked_all.transpose(1, 0, 2, 3).reshape(2048, 128)

    def diagonal(values, width):
        count = values.shape[1] // width
        column = jnp.arange(values.shape[1]) // width
        row = jnp.arange(count * RANK) // RANK
        tiled = jnp.concatenate([values] * count, axis=0)
        return jnp.where(row[:, None] == column[None, :], tiled, 0).astype(B16)

    half = jnp.asarray(ADAPTER_SCALING, B16)
    pad_rank = lambda v: jnp.pad(v, ((0, 0), (0, 128 - v.shape[1])))

    seq_normed_one = [
        jnp.concatenate([normed_one_b, core_normed], axis=0),
        jnp.concatenate([far_normed, send(far_normed, CORES)], axis=0),
    ]
    seq_upstream = [
        jnp.concatenate([upstream_b, core_upstream], axis=0),
        jnp.concatenate([far_upstream, send(far_upstream, CORES)], axis=0),
    ]

    def by_core(pair):
        return [jnp.concatenate([v[:rows] for v in pair]), jnp.concatenate([v[rows:] for v in pair])]

    lowrank_inputs = [product(v, picked_wide).astype(B16)[:, 0:48] for v in seq_normed_one]
    diag_in = diagonal(pick_attention[:, : 3 * proj], proj)
    projected = [
        (product(v, w_in) + product(low * half, diag_in)).astype(B16)
        for v, low in zip(seq_normed_one, lowrank_inputs)
    ]
    attention_b, raw, lse, qkv = attention_forward(
        own_quarter, lambda_all, projected[0], projected[1], heads_local
    )
    pick_out = pick_attention[:, 3 * proj :]

    def partial_sum(values, weights, low, scaling, form="lc,dc->ld"):
        return jnp.concatenate(
            [
                contract(form, values, weights),
                pad_rank(scaling * contract("lc,rc->lr", values, low)),
            ],
            axis=1,
        )

    halves = by_core([attention_b[: 2 * rows], attention_b[2 * rows :]])
    out_sum = scatter_tokens(
        *[lambda v=v: partial_sum(v, w_out, pick_out, 1.0) for v in halves]
    )
    lowrank_out_b = out_sum[:, 2048 : 2048 + RANK].astype(B16)
    residual_one = (
        local_tokens
        + out_sum[:, :2048]
        + contract("tr,dr->td", lowrank_out_b * half, picked_wide[:, 80:96])
    )

    def gather_tokens(values):
        core, far_values = send(values, CORES), send(values, FAR_X)
        return [
            jnp.concatenate([values, core], axis=0),
            jnp.concatenate([far_values, send(far_values, CORES)], axis=0),
        ]

    second_normalized, scale_two = norm_forward(residual_one, gain_values[1])
    normed_two_b = second_normalized.astype(B16)
    seq_normed_two = gather_tokens(normed_two_b)
    lowrank_hidden = [product(v, picked_wide).astype(B16)[:, 48:80] for v in seq_normed_two]
    diag_hidden = diagonal(pick_hidden, ff)
    gate_up = [
        product(v, w_hidden) + product(low * half, diag_hidden)
        for v, low in zip(seq_normed_two, lowrank_hidden)
    ]
    hidden_b = [(jax.nn.silu(v[:, :ff]) * v[:, ff:]).astype(B16) for v in gate_up]
    down_sum = scatter_tokens(
        *[lambda v=v: partial_sum(v, w_down, pick_down, 1.0) for v in by_core(hidden_b)]
    )
    lowrank_down_b = down_sum[:, 2048 : 2048 + RANK].astype(B16)
    result = (
        residual_one
        + down_sum[:, :2048]
        + contract("tr,dr->td", lowrank_down_b * half, picked_wide[:, 96:112])
    )

    grad_right_down = ADAPTER_SCALING * contract("td,tr->dr", upstream_b, lowrank_down_b)
    grad_lowrank_down = [
        (ADAPTER_SCALING * product(v, picked_wide)).astype(B16)[:, 96:112] for v in seq_upstream
    ]
    grad_gate_up = []
    for v, low, gates in zip(seq_upstream, grad_lowrank_down, gate_up):
        grad_hidden = product(v, w_down) + product(low, pick_down)
        gate, upper = gates[:, :ff], gates[:, ff:]
        sigmoid_gate = jax.nn.sigmoid(gate)
        grad_gate = grad_hidden * upper * sigmoid_gate * (1.0 + gate * (1.0 - sigmoid_gate))
        grad_upper = grad_hidden * gate * sigmoid_gate
        grad_gate_up.append(
            jnp.concatenate([grad_gate.astype(B16), grad_upper.astype(B16)], axis=1)
        )

    def token_sum(left, right):
        return sum(contract("lr,lc->rc", a, b) for a, b in zip(left, right))

    grad_left_down = token_sum(grad_lowrank_down, hidden_b)
    right_hidden = [
        ADAPTER_SCALING
        * token_sum(
            [v[:, RANK * i : RANK * (i + 1)] for v in lowrank_hidden],
            [v[:, ff * i : ff * (i + 1)] for v in grad_gate_up],
        )
        for i in range(2)
    ]
    hidden_sum = scatter_tokens(
        *[
            lambda v=v: partial_sum(v, w_hidden, diag_hidden, ADAPTER_SCALING)
            for v in by_core(grad_gate_up)
        ]
    )
    grad_lowrank_hidden = hidden_sum[:, 2048 : 2048 + 2 * RANK].astype(B16)
    grad_left_hidden = contract("td,tr->dr", normed_two_b, grad_lowrank_hidden)
    grad_normed_two = hidden_sum[:, :2048] + contract(
        "tr,dr->td", grad_lowrank_hidden, picked_wide[:, 48:80]
    )
    grad_residual = upstream_b.astype(F32) + norm_backward(
        residual_one, scale_two, gain_values[1], grad_normed_two
    )

    grad_branch_b = grad_residual.astype(B16)
    grad_right_out = ADAPTER_SCALING * contract("td,tr->dr", grad_branch_b, lowrank_out_b)
    seq_grad_branch = gather_tokens(grad_branch_b)
    grad_lowrank_out = [
        (ADAPTER_SCALING * product(v, picked_wide)).astype(B16)[:, 80:96] for v in seq_grad_branch
    ]
    grad_attention_in = [
        product(v, w_out) + product(low, pick_out)
        for v, low in zip(seq_grad_branch, grad_lowrank_out)
    ]
    grad_left_out = token_sum(
        grad_lowrank_out, [attention_b[: 2 * rows], attention_b[2 * rows :]]
    )
    grad_projected = attention_backward(
        own_quarter, lambda_all, qkv, raw, lse, *grad_attention_in, heads_local
    )
    grad_projected_pair = [grad_projected[: 2 * rows], grad_projected[2 * rows :]]
    right_inputs = [
        ADAPTER_SCALING
        * token_sum(
            [v[:, RANK * i : RANK * (i + 1)] for v in lowrank_inputs],
            [v[:, proj * i : proj * (i + 1)] for v in grad_projected_pair],
        )
        for i in range(3)
    ]
    input_sum = scatter_tokens(
        *[
            lambda v=v: partial_sum(v, w_in, diag_in, ADAPTER_SCALING)
            for v in by_core(grad_projected_pair)
        ]
    )
    grad_lowrank_inputs = input_sum[:, 2048 : 2048 + 3 * RANK].astype(B16)
    grad_left_inputs = contract("td,tr->dr", normed_one_b, grad_lowrank_inputs)
    grad_normed_one = input_sum[:, :2048] + contract(
        "tr,dr->td", grad_lowrank_inputs, picked_wide[:, 0:48]
    )
    grad_input = grad_residual + norm_backward(
        local_tokens, scale_one, gain_values[0], grad_normed_one
    )

    wide_grads = jnp.concatenate(
        [
            grad_left_inputs,
            grad_left_hidden,
            grad_right_out,
            grad_right_down,
            jnp.zeros((2048, RANK), F32),
        ],
        axis=1,
    ).astype(B16)
    split_grads = jnp.concatenate(
        right_inputs + [grad_left_out] + right_hidden + [grad_left_down], axis=1
    ).astype(B16)
    columns = split_grads.shape[1]
    piece = -(-columns // 1024) * 128
    split_blocks = (
        jnp.pad(split_grads, ((0, 0), (0, 8 * piece - columns)))
        .reshape(4, 4, 2, 4, piece)
        .transpose(1, 2, 0, 3, 4)
        .reshape(128, piece // 128, 128)
    )
    blocks = jnp.concatenate(
        [
            wide_grads.reshape(128, 16, 128),
            split_blocks,
            jnp.broadcast_to(adapter.astype(B16), (128, 8 - piece // 128, 128)),
        ],
        axis=1,
    )
    arrived = lax.all_to_all(blocks, AXES, split_axis=0, concat_axis=0, tiled=True)
    ids_all = arrived.reshape(32, 4, 24, 128)[:, 0, 23, 0].astype(jnp.int32)
    member = ids_all[None, :] == jnp.arange(ADAPTERS)[:, None]
    onehot = member.astype(B16)
    wide_sum = contract(
        "es,sn->en",
        onehot,
        arrived[:, :16].reshape(32, 4 * 16 * 128),
    ).reshape(8, 4, 16, 128).sum(1)
    split_sum = contract(
        "es,sn->en", onehot, arrived[:, 16:].reshape(32, 4 * 8 * 128)
    ).reshape(8, 4, 8, 128)[:, :, : piece // 128]
    squares = jnp.sum(wide_sum * wide_sum) + jnp.sum(split_sum * split_sum)
    grads_wide = (
        wide_sum[:, :, :112].reshape(8, 16, 7, 16).transpose(2, 0, 3, 1).reshape(7, 128, 16)
    )
    mine = place.dp % 4
    split_out = jnp.concatenate(
        [split_sum.reshape(32, 7, 128), jnp.zeros((32, 1, 128), F32)], axis=1
    ).reshape(8, 1, 4, 8, 128)
    quarter = jnp.arange(4)[None, :, None, None, None]
    spread = jnp.where(quarter == mine, split_out, 0.0).reshape(128, 8, 128)
    spread = jnp.where(jnp.arange(8)[None, :, None] == 7, squares, spread)
    placed = lax.all_to_all(spread, AXES, split_axis=0, concat_axis=0, tiled=True)
    total_squares = jnp.sum(placed[:, 7, 0])
    from_mine = lax.dynamic_index_in_dim(
        placed.reshape(8, 4, 4, 8, 128), mine, 1, keepdims=False
    )
    split_rows = from_mine[:, :, :7].reshape(4, 8 * piece)[:, :columns]
    grads_attention = split_rows[:, : 4 * proj].reshape(4, 4, proj).transpose(1, 0, 2)
    grads_feedforward = split_rows[:, 4 * proj :].reshape(4, 3, ff).transpose(1, 0, 2)

    grad_norm = jnp.sqrt(total_squares)
    factor = CLIP_NORM / (grad_norm + 1e-06)
    wide_new = adam_step(adapter_wide, grads_wide, moment_wide, variance_wide, factor)
    attention_new = adam_step(
        adapter_attention, grads_attention, moment_attention, variance_attention, factor
    )
    feedforward_new = adam_step(
        adapter_feedforward, grads_feedforward, moment_feedforward, variance_feedforward, factor
    )
    return (
        result.astype(B16)[None],
        grad_input.astype(B16)[None],
        grad_norm,
        wide_new[0],
        attention_new[0],
        feedforward_new[0],
        wide_new[1],
        attention_new[1],
        feedforward_new[1],
        wide_new[2],
        attention_new[2],
        feedforward_new[2],
        wide_new[3],
        attention_new[3],
        feedforward_new[3],
    )


def solution(mesh):
    return jax.shard_map(
        local,
        mesh=mesh,
        in_specs=(
            P("dp", "tensor", None),
            P("dp", "tensor", None),
            P("dp"),
            P(),
            P(None, "tensor", None),
            P(None, "dp", "tensor"),
            P("tensor", "dp"),
            P(None, "dp", "tensor"),
            P("tensor", "dp"),
            P(None, None, ("dp", "tensor")),
            P(None, "dp", "tensor"),
            P(None, "dp", "tensor"),
            P(None, None, ("dp", "tensor")),
            P(None, None, ("dp", "tensor")),
            P(None, "dp", "tensor"),
            P(None, "dp", "tensor"),
            P(None, "dp", "tensor"),
            P(None, "dp", "tensor"),
        ),
        out_specs=(
            P("dp", "tensor", None),
            P("dp", "tensor", None),
            P(),
            P(None, None, ("dp", "tensor")),
            P(None, "dp", "tensor"),
            P(None, "dp", "tensor"),
            P(None, None, ("dp", "tensor")),
            P(None, "dp", "tensor"),
            P(None, "dp", "tensor"),
            P(None, None, ("dp", "tensor")),
            P(None, "dp", "tensor"),
            P(None, "dp", "tensor"),
            P(None, None, ("dp", "tensor")),
            P(None, "dp", "tensor"),
            P(None, "dp", "tensor"),
        ),
        check_vma=False,
    )
```

time: 845 us -> 1430 us (1.69)
  Pallas kernels: 0 us -> 888 us
  waiting for transfers between devices: 300 us -> 180 us
  local copies, waits for them, and re-layouts: 176 us -> 68.7 us
  matrix products: 168 us -> 132 us
  other arithmetic: 55.8 us -> 35.5 us
  starting transfers between devices: 125 us -> 109 us
    pallas_call x0 -> x4, Pallas kernels: none -> 888 us  [the longest x2 876 us: assemble(): pl.pallas_call(kernel, out_shape=[jax.ShapeDtypeStruct((rows, width), B16...]
    ppermute x68 -> x57, waiting for transfers between devices: 280 us -> 159 us  [send(): return lax.ppermute(values, AXES, pairs)]
    dynamic_update_slice x118 -> x0, local copies, waits for them, and re-layouts: 89.7 us -> none  [put(): return lax.dynamic_update_slice(buffer, values, starts)]
    dot_general x36 -> x39, matrix products: 107 us -> 72.9 us  [contract(): return jnp.einsum(form, left, right, preferred_element_type=F32)]
    ppermute x68 -> x57, starting transfers between devices: 112 us -> 95.6 us  [send(): return lax.ppermute(values, AXES, pairs)]
    dot_general x15 -> x25, matrix products: 60.6 us -> 58.6 us  [product(): return jnp.dot(left, right, preferred_element_type=F32)]
  transfers between devices with their start and end apart: 70 -> 59, of which waited for: 39 -> 25; matrix products, arithmetic and copies ran while one was open for 35% -> 9% of each run, Pallas kernels for 0% -> 22%
where the time goes in v2:
time: 1430 us; the launch traced here: 1420 us
  Pallas kernels  888 us (62%)
  waiting for transfers between devices  180 us (13%)
  matrix products  132 us (9%)
  starting transfers between devices  109 us (8%)
  local copies, waits for them, and re-layouts  68.7 us (5%)
  other arithmetic  35.5 us (2%)
    pallas_call x2, Pallas kernels, assemble(): pl.pallas_call(kernel, out_shape=[jax.ShapeDtypeStruct((rows, width), B16...  876 us
    ppermute x57, waiting for transfers between devices, send(): return lax.ppermute(values, AXES, pairs)  159 us
    ppermute x57, starting transfers between devices, send(): return lax.ppermute(values, AXES, pairs)  95.6 us
    dot_general x39, matrix products, contract(): return jnp.einsum(form, left, right, preferred_element_type=F32)  72.9 us
    dot_general x25, matrix products, product(): return jnp.dot(left, right, preferred_element_type=F32)  58.6 us
  transfers between devices with their start and end apart: 59, of which 25 were waited for; matrix products, arithmetic and copies ran while one was open for 9% of the time, Pallas kernels for 22%

profile of v2, /device:TPU:1, one launch (start us, length us, event | category | flops | bytes accessed | tf_op | source)
XLA Modules:
  0.0 1420.6 jit_solution(13706785966394173223)
XLA Ops:
  8.6 6.6 collective-permute-done
  28.5 7.1 collective-permute-done.6
  57.2 14.7 %collective-permute-done.16 = bf16[192,2048]{1,0:T(8,128)(2,1)} collective-permute-done((bf16[192,2048]{1,0:T(8,128)(2,1)S(1)}, bf16[192,2048]{1,0:T(8,128)(2,1)}, u32[]{:S(2)}, u32[]{:S(2)}) %collective-permute-start.16) | collective-permute-done | bytes 786464 | tf_op jit(solution)/shard_map/ppermute | solution.py:66
  105.8 302.9 %shard_map.289 = (bf16[2048,1536]{1,0:T(8,128)(2,1)}, bf16[2048,512]{1,0:T(8,128)(2,1)}, bf16[2048,384]{1,0:T(8,128)(2,1)}) custom-call(bf16[8,32,2432]{2,1,0:T(8,128)(2,1)} %copy-done.49, bf16[8,32,2432]{2,1,0:T(8,128)(2,1)} %copy-done.40, bf16[8,32,2432]{2,1,0:T(8,128)(2,1)} %copy-done.41, bf16[4,32,2432]{2,1,0:T(8,128)(2,1)} %collective-permute-done.17.refs_3_, ...), custom_call_target="tpu_custom_call" | custom-call | bytes 19922944 | tf_op jit(solution)/shard_map/pallas_call | solution.py:116
  414.0 5.7 collective-permute-start.24
  480.7 15.3 %collective-permute-done.27 = bf16[192,2176]{1,0:T(8,128)(2,1)S(1)} collective-permute-done((bf16[192,2176]{1,0:T(8,128)(2,1)S(1)}, bf16[192,2176]{1,0:T(8,128)(2,1)S(1)}, u32[]{:S(2)}, u32[]{:S(2)}) %collective-permute-start.27) | collective-permute-done | bytes 835616 | tf_op jit(solution)/shard_map/ppermute | solution.py:66
  502.0 23.9 %collective-permute-done.39.refs_6_ = bf16[8,32,4608]{2,1,0:T(8,128)(2,1)S(1)} collective-permute-done((bf16[8,32,4608]{2,1,0:T(8,128)(2,1)}, bf16[8,32,4608]{2,1,0:T(8,128)(2,1)S(1)}, u32[]{:S(2)}, u32[]{:S(2)}) %collective-permute-start.39) | collective-permute-done | bytes 2359328 | tf_op jit(solution)/shard_map/ppermute | solution.py:66
  532.2 13.4 collective-permute-done.38.refs_2_
  556.3 13.9 collective-permute-done.41.refs_3_
  572.7 572.9 %shard_map.291 = (bf16[2048,2816]{1,0:T(8,128)(2,1)}, bf16[2048,1408]{1,0:T(8,128)(2,1)}, bf16[2048,384]{1,0:T(8,128)(2,1)}) custom-call(bf16[8,32,4608]{2,1,0:T(8,128)(2,1)} %constant_dynamic-update-slice_fusion.21.refs_0_, bf16[8,32,4608]{2,1,0:T(8,128)(2,1)} %copy-done.23, bf16[8,32,4608]{2,1,0:T(8,128)(2,1)} %copy-done.24, ...), custom_call_target="tpu_custom_call" | custom-call | bytes 37748736 | tf_op jit(solution)/shard_map/pallas_call | solution.py:116
  1151.4 10.7 convolution_add_fusion
  1162.1 10.2 convolution_add_fusion.1
  1172.3 6.9 multiply_convert_fusion.2
  1182.8 13.9 convolution_convert_fusion
  1212.9 6.1 collective-permute-start.50
  1222.1 7.5 fusion.44
  1241.4 17.9 %collective-permute-done.51 = bf16[192,2176]{1,0:T(8,128)(2,1)S(1)} collective-permute-done((bf16[192,2176]{1,0:T(8,128)(2,1)S(1)}, bf16[192,2176]{1,0:T(8,128)(2,1)S(1)}, u32[]{:S(2)}, u32[]{:S(2)}) %collective-permute-start.51) | collective-permute-done | bytes 835616 | tf_op jit(solution)/shard_map/ppermute | solution.py:66
  1267.1 10.1 collective-permute-done.48
  1287.3 6.8 collective-permute-done.53
  1304.0 7.7 shard_map.292
  1351.3 7.2 collective-permute-done.56
  1362.6 9.1 all-to-all-start
  1377.8 9.9 all-to-all-done
  1404.2 10.3 all-to-all-done.1
  (605 shorter events, 302.6 us)
Async XLA Ops:
  48.5 28.4 %collective-permute-start.14 = (bf16[8,32,2432]{2,1,0:T(8,128)(2,1)S(1)}, bf16[8,32,2432]{2,1,0:T(8,128)(2,1)S(1)}, u32[]{:S(2)}, u32[]{:S(2)}) collective-permute-start(bf16[8,32,2432]{2,1,0:T(8,128)(2,1)S(1)} %constant_dynamic-update-slice_fusion.13.refs_5_), channel_id=1, source_target_pairs={{0,8},{1,9},{4,12},{5,13},{2,10},{3,11},{6,14},{7,15},{8,16},{9,17... | collective-permute-start | bytes 3735560 | tf_op jit(solution)/shard_map/ppermute | solution.py:66
  48.5 28.3 %collective-permute-start.15 = (bf16[8,32,2432]{2,1,0:T(8,128)(2,1)S(1)}, bf16[8,32,2432]{2,1,0:T(8,128)(2,1)S(1)}, u32[]{:S(2)}, u32[]{:S(2)}) collective-permute-start(bf16[8,32,2432]{2,1,0:T(8,128)(2,1)S(1)} %constant_dynamic-update-slice_fusion.13.refs_5_), channel_id=1, source_target_pairs={{0,24},{1,25},{4,28},{5,29},{2,26},{3,27},{6,30},{7,31},{8,0},{9,1... | collective-permute-start | bytes 3735560 | tf_op jit(solution)/shard_map/ppermute | solution.py:66
  51.3 27.8 %collective-permute-start.12 = (bf16[8,32,2432]{2,1,0:T(8,128)(2,1)S(1)}, bf16[8,32,2432]{2,1,0:T(8,128)(2,1)S(1)}, u32[]{:S(2)}, u32[]{:S(2)}) collective-permute-start(bf16[8,32,2432]{2,1,0:T(8,128)(2,1)S(1)} %constant_dynamic-update-slice_fusion.7.refs_0_), channel_id=1, source_target_pairs={{0,32},{1,33},{4,36},{5,37},{2,34},{3,35},{6,38},{7,39},{8,40},{9,... | collective-permute-start | bytes 3735560 | tf_op jit(solution)/shard_map/ppermute | solution.py:66
  51.3 27.8 %collective-permute-start.13 = (bf16[8,32,2432]{2,1,0:T(8,128)(2,1)S(1)}, bf16[8,32,2432]{2,1,0:T(8,128)(2,1)S(1)}, u32[]{:S(2)}, u32[]{:S(2)}) collective-permute-start(bf16[8,32,2432]{2,1,0:T(8,128)(2,1)S(1)} %constant_dynamic-update-slice_fusion.7.refs_0_), channel_id=1, source_target_pairs={{0,96},{1,97},{4,100},{5,101},{2,98},{3,99},{6,102},{7,103},{8,104... | collective-permute-start | bytes 3735560 | tf_op jit(solution)/shard_map/ppermute | solution.py:66
  96.4 331.3 %collective-permute-start.25 = (bf16[192,2048]{1,0:T(8,128)(2,1)}, bf16[192,2048]{1,0:T(8,128)(2,1)}, u32[]{:S(2)}, u32[]{:S(2)}) collective-permute-start(bf16[192,2048]{1,0:T(8,128)(2,1)} %collective-permute-done.16), channel_id=1, source_target_pairs={{0,1},{1,0},{4,5},{5,4},{2,3},{3,2},{6,7},{7,6},{8,9},{9,8},{12,13... | collective-permute-start | bytes 2359304 | tf_op jit(solution)/shard_map/ppermute | solution.py:66
  101.8 350.8 %collective-permute-start.29 = (bf16[2,32,4608]{2,1,0:T(8,128)(2,1)}, bf16[2,32,4608]{2,1,0:T(8,128)(2,1)}, u32[]{:S(2)}, u32[]{:S(2)}) collective-permute-start(bf16[2,32,4608]{2,1,0:T(8,128)(2,1)} %pad_maximum_fusion.28), channel_id=1, source_target_pairs={{0,8},{1,9},{4,12},{5,13},{2,10},{3,11},{6,14},{7,15},{8,16},{9,17... | collective-permute-start | bytes 1769480 | tf_op jit(solution)/shard_map/ppermute | solution.py:66
  101.8 350.8 %collective-permute-start.30 = (bf16[2,32,4608]{2,1,0:T(8,128)(2,1)}, bf16[2,32,4608]{2,1,0:T(8,128)(2,1)}, u32[]{:S(2)}, u32[]{:S(2)}) collective-permute-start(bf16[2,32,4608]{2,1,0:T(8,128)(2,1)} %pad_maximum_fusion.28), channel_id=1, source_target_pairs={{0,24},{1,25},{4,28},{5,29},{2,26},{3,27},{6,30},{7,31},{8,0},{9,1... | collective-permute-start | bytes 1769480 | tf_op jit(solution)/shard_map/ppermute | solution.py:66
  427.7 24.9 %collective-permute-start.31 = (bf16[2,32,4608]{2,1,0:T(8,128)(2,1)}, bf16[2,32,4608]{2,1,0:T(8,128)(2,1)}, u32[]{:S(2)}, u32[]{:S(2)}) collective-permute-start(bf16[2,32,4608]{2,1,0:T(8,128)(2,1)} %pad_maximum_fusion.29), channel_id=1, source_target_pairs={{0,32},{1,33},{4,36},{5,37},{2,34},{3,35},{6,38},{7,39},{8,40},{9,... | collective-permute-start | bytes 1769480 | tf_op jit(solution)/shard_map/ppermute | solution.py:66
  429.2 23.4 %collective-permute-start.32 = (bf16[2,32,4608]{2,1,0:T(8,128)(2,1)}, bf16[2,32,4608]{2,1,0:T(8,128)(2,1)}, u32[]{:S(2)}, u32[]{:S(2)}) collective-permute-start(bf16[2,32,4608]{2,1,0:T(8,128)(2,1)} %pad_maximum_fusion.29), channel_id=1, source_target_pairs={{0,96},{1,97},{4,100},{5,101},{2,98},{3,99},{6,102},{7,103},{8,104... | collective-permute-start | bytes 1769480 | tf_op jit(solution)/shard_map/ppermute | solution.py:66
  450.1 26.2 %collective-permute-start.26 = (bf16[384,2176]{1,0:T(8,128)(2,1)S(1)}, bf16[384,2176]{1,0:T(8,128)(2,1)S(1)}, u32[]{:S(2)}, u32[]{:S(2)}) collective-permute-start(bf16[384,2176]{1,0:T(8,128)(2,1)S(1)} %fusion.26), channel_id=1, source_target_pairs={{0,1},{1,0},{4,5},{5,4},{2,3},{3,2},{6,7},{7,6},{8,9},{9,8},{12,13... | collective-permute-start | bytes 5013512 | tf_op jit(solution)/shard_map/ppermute | solution.py:66
  469.8 29.7 %collective-permute-start.49 = (bf16[192,2048]{1,0:T(8,128)(2,1)}, bf16[192,2048]{1,0:T(8,128)(2,1)S(1)}, u32[]{:S(2)}, u32[]{:S(2)}) collective-permute-start(bf16[192,2048]{1,0:T(8,128)(2,1)} %collective-permute-done.21), channel_id=1, source_target_pairs={{0,1},{1,0},{4,5},{5,4},{2,3},{3,2},{6,7},{7,6},{8,9},{9,8},{12,13... | collective-permute-start | bytes 2359304 | tf_op jit(solution)/shard_map/ppermute | solution.py:66
  473.6 52.3 %collective-permute-start.39 = (bf16[8,32,4608]{2,1,0:T(8,128)(2,1)}, bf16[8,32,4608]{2,1,0:T(8,128)(2,1)S(1)}, u32[]{:S(2)}, u32[]{:S(2)}) collective-permute-start(bf16[8,32,4608]{2,1,0:T(8,128)(2,1)} %constant_dynamic-update-slice_fusion.27.refs_5_), channel_id=1, source_target_pairs={{0,8},{1,9},{4,12},{5,13},{2,10},{3,11},{6,14},{7,15},{8,16},{9,17... | collective-permute-start | bytes 7077896 | tf_op jit(solution)/shard_map/ppermute | solution.py:66
  473.6 58.5 %collective-permute-start.40 = (bf16[8,32,4608]{2,1,0:T(8,128)(2,1)}, bf16[8,32,4608]{2,1,0:T(8,128)(2,1)S(1)}, u32[]{:S(2)}, u32[]{:S(2)}) collective-permute-start(bf16[8,32,4608]{2,1,0:T(8,128)(2,1)} %constant_dynamic-update-slice_fusion.27.refs_5_), channel_id=1, source_target_pairs={{0,24},{1,25},{4,28},{5,29},{2,26},{3,27},{6,30},{7,31},{8,0},{9,1... | collective-permute-start | bytes 7077896 | tf_op jit(solution)/shard_map/ppermute | solution.py:66
  480.7 51.5 %collective-permute-start.37 = (bf16[8,32,4608]{2,1,0:T(8,128)(2,1)}, bf16[8,32,4608]{2,1,0:T(8,128)(2,1)S(1)}, u32[]{:S(2)}, u32[]{:S(2)}) collective-permute-start(bf16[8,32,4608]{2,1,0:T(8,128)(2,1)} %constant_dynamic-update-slice_fusion.21.refs_0_), channel_id=1, source_target_pairs={{0,32},{1,33},{4,36},{5,37},{2,34},{3,35},{6,38},{7,39},{8,40},{9,... | collective-permute-start | bytes 7077896 | tf_op jit(solution)/shard_map/ppermute | solution.py:66
  496.0 49.6 %collective-permute-start.38 = (bf16[8,32,4608]{2,1,0:T(8,128)(2,1)}, bf16[8,32,4608]{2,1,0:T(8,128)(2,1)S(1)}, u32[]{:S(2)}, u32[]{:S(2)}) collective-permute-start(bf16[8,32,4608]{2,1,0:T(8,128)(2,1)} %constant_dynamic-update-slice_fusion.21.refs_0_), channel_id=1, source_target_pairs={{0,96},{1,97},{4,100},{5,101},{2,98},{3,99},{6,102},{7,103},{8,104... | collective-permute-start | bytes 7077896 | tf_op jit(solution)/shard_map/ppermute | solution.py:66
  499.5 32.4 %collective-permute-start.45 = (bf16[192,2048]{1,0:T(8,128)(2,1)S(1)}, bf16[192,2048]{1,0:T(8,128)(2,1)S(1)}, u32[]{:S(2)}, u32[]{:S(2)}) collective-permute-start(bf16[192,2048]{1,0:T(8,128)(2,1)S(1)} %multiply_convert_fusion.6), channel_id=1, source_target_pairs={{0,2},{1,3},{4,6},{5,7},{2,0},{3,1},{6,4},{7,5},{8,10},{9,11},{12,... | collective-permute-start | bytes 2359304 | tf_op jit(solution)/shard_map/ppermute | solution.py:66
  545.7 24.5 %collective-permute-start.41 = (bf16[4,32,4608]{2,1,0:T(8,128)(2,1)S(1)}, bf16[4,32,4608]{2,1,0:T(8,128)(2,1)}, u32[]{:S(2)}, u32[]{:S(2)}) collective-permute-start(bf16[4,32,4608]{2,1,0:T(8,128)(2,1)S(1)} %slice.455), channel_id=1, source_target_pairs={{0,32},{1,33},{4,36},{5,37},{2,34},{3,35},{6,38},{7,39},{8,40},{9,... | collective-permute-start | bytes 3538952 | tf_op jit(solution)/shard_map/ppermute | solution.py:66
  545.9 24.4 %collective-permute-start.42 = (bf16[4,32,4608]{2,1,0:T(8,128)(2,1)S(1)}, bf16[4,32,4608]{2,1,0:T(8,128)(2,1)}, u32[]{:S(2)}, u32[]{:S(2)}) collective-permute-start(bf16[4,32,4608]{2,1,0:T(8,128)(2,1)S(1)} %slice.456), channel_id=1, source_target_pairs={{0,96},{1,97},{4,100},{5,101},{2,98},{3,99},{6,102},{7,103},{8,104... | collective-permute-start | bytes 3538952 | tf_op jit(solution)/shard_map/ppermute | solution.py:66
  549.0 23.7 %collective-permute-start.43 = (bf16[4,32,4608]{2,1,0:T(8,128)(2,1)S(1)}, bf16[4,32,4608]{2,1,0:T(8,128)(2,1)}, u32[]{:S(2)}, u32[]{:S(2)}) collective-permute-start(bf16[4,32,4608]{2,1,0:T(8,128)(2,1)S(1)} %slice.457), channel_id=1, source_target_pairs={{0,8},{1,9},{4,12},{5,13},{2,10},{3,11},{6,14},{7,15},{8,16},{9,17... | collective-permute-start | bytes 3538952 | tf_op jit(solution)/shard_map/ppermute | solution.py:66
  549.2 23.5 %collective-permute-start.44 = (bf16[4,32,4608]{2,1,0:T(8,128)(2,1)S(1)}, bf16[4,32,4608]{2,1,0:T(8,128)(2,1)}, u32[]{:S(2)}, u32[]{:S(2)}) collective-permute-start(bf16[4,32,4608]{2,1,0:T(8,128)(2,1)S(1)} %slice.458), channel_id=1, source_target_pairs={{0,24},{1,25},{4,28},{5,29},{2,26},{3,27},{6,30},{7,31},{8,0},{9,1... | collective-permute-start | bytes 3538952 | tf_op jit(solution)/shard_map/ppermute | solution.py:66
  1240.8 36.4 %collective-permute-start.48 = (bf16[192,2176]{1,0:T(8,128)(2,1)S(1)}, bf16[192,2176]{1,0:T(8,128)(2,1)S(1)}, u32[]{:S(2)}, u32[]{:S(2)}) collective-permute-start(bf16[192,2176]{1,0:T(8,128)(2,1)S(1)} %slice.803), channel_id=1, source_target_pairs={{0,2},{1,3},{4,6},{5,7},{2,0},{3,1},{6,4},{7,5},{8,10},{9,11},{12,... | collective-permute-start | bytes 2506760 | tf_op jit(solution)/shard_map/ppermute | solution.py:66
  1262.5 31.6 %collective-permute-start.53 = (bf16[192,2048]{1,0:T(8,128)(2,1)}, bf16[192,2048]{1,0:T(8,128)(2,1)}, u32[]{:S(2)}, u32[]{:S(2)}) collective-permute-start(bf16[192,2048]{1,0:T(8,128)(2,1)} %fusion.203), channel_id=1, source_target_pairs={{0,2},{1,3},{4,6},{5,7},{2,0},{3,1},{6,4},{7,5},{8,10},{9,11},{12,... | collective-permute-start | bytes 2359304 | tf_op jit(solution)/shard_map/ppermute | solution.py:66
  1265.0 31.6 %collective-permute-start.52 = (bf16[192,2048]{1,0:T(8,128)(2,1)}, bf16[192,2048]{1,0:T(8,128)(2,1)}, u32[]{:S(2)}, u32[]{:S(2)}) collective-permute-start(bf16[192,2048]{1,0:T(8,128)(2,1)} %fusion.203), channel_id=1, source_target_pairs={{0,1},{1,0},{4,5},{5,4},{2,3},{3,2},{6,7},{7,6},{8,9},{9,8},{12,13... | collective-permute-start | bytes 2359304 | tf_op jit(solution)/shard_map/ppermute | solution.py:66
  1362.6 25.1 %all-to-all-start = ((bf16[128,24,128]{2,1,0:T(8,128)(2,1)}), bf16[128,24,128]{2,1,0:T(8,128)(2,1)}, u32[]{:S(2)}, u32[]{:S(2)}) async-start(bf16[128,24,128]{2,1,0:T(8,128)(2,1)} %copy.164), calls=%async_computation | async-start | bytes 1572864 | tf_op jit(solution)/shard_map/all_to_all | solution.py:704
  (161 other events, 6419.3 us)
